TPU v7x, 256 devices: a whole 4x4x8 slice. The times are simulated.
256 devices in a mesh: row: 8 (over z_hi, core), col: 32 (over z_lo, y, x).
Axes of the slice: x: 4, y: 4, z: 8 (z_hi: 4, z_lo: 2; z = z_hi * 2 + z_lo), core: 2. Of those that a mesh axis runs over, the one named last changes fastest.
Arguments:
- local_copy: float32 [2, 5120, 12288], P(None, 'row', 'col'), may hold values from -5 to 5
- dual: float32 [2, 5120, 12288], P(None, 'row', 'col'), may hold values from -4 to 4
- consensus: float32 [2, 4096, 8192], P(None, 'row', 'col'), may hold values from -5 to 5
- probe: float32 [2, 128, 128], replicated, may hold values from -6 to 6
- intensity: float32 [8192, 128, 128], P(('row', 'col')), may hold values from 0.1 to 24, as said below
- pos_rows: int32 [8192], P(('row', 'col')), may hold values from 0 to 4095, as said below
- pos_cols: int32 [8192], P(('row', 'col')), may hold values from 0 to 8191, as said below
Outputs:
- new_copy: float32 [2, 5120, 12288], P(None, 'row', 'col')
- new_consensus: float32 [2, 4096, 8192], P(None, 'row', 'col')
- new_dual: float32 [2, 5120, 12288], P(None, 'row', 'col')
- new_probe: float32 [2, 128, 128], replicated
Inputs may be any that keep to these rules, and one draw needn't show every extreme that they name: `pos_rows`: pattern j starts in the rows of tile j // 32, tiles numbered a * 32 + b; in every tile one pattern starts on the tile's last row. `pos_cols`: pattern j starts in the columns of tile j // 32; in every tile one pattern starts on the tile's last column. `intensity`: Positive.
All inputs are finite; a program needn't handle non-finite values.
Results may differ from a plain program's by a relative error of at most 0.000065.
Values sent between devices are 32-bit elements; how exact they have to be, the bound alone decides.
A program may use at most 64 MiB of HBM per device.

v0:
```python
import math

import jax
import jax.numpy as jnp
from jax import lax
from jax.sharding import PartitionSpec as P

PATCH_BLOCK = 4


object_step = 0.3
penalty = 1.0
probe_step = 0.5
epsilon = 1e-06


def passed_along(value, axis, steps):
    count = lax.axis_size(axis)
    first, last = (max(0, -steps), min(count, count - steps))
    return lax.ppermute(value, axis, [(source, source + steps) for source in range(first, last)])


def dft_tables(patch_side):
    indices = jnp.arange(patch_side, dtype=jnp.int32)
    phases = indices[:, None] * indices[None, :] % patch_side
    angles = phases.astype(jnp.float32) * (2.0 * math.pi / patch_side)
    norm_factor = 1.0 / math.sqrt(patch_side)
    return (jnp.cos(angles) * norm_factor, jnp.sin(angles) * norm_factor)


def times_right(values, table):
    return jnp.einsum("bij,jk->bik", values, table, precision=lax.Precision.HIGHEST)


def times_left(table, values):
    return jnp.einsum("ij,bjk->bik", table, values, precision=lax.Precision.HIGHEST)


def transform(real_part, imag_part, cosine, sine, direction):
    first_re = times_right(real_part, cosine) + direction * times_right(imag_part, sine)
    first_im = times_right(imag_part, cosine) - direction * times_right(real_part, sine)
    second_re = times_left(cosine, first_re) + direction * times_left(sine, first_im)
    second_im = times_left(cosine, first_im) - direction * times_left(sine, first_re)
    return (second_re, second_im)


def per_device(local_copy, dual, consensus, probe, intensity, pos_rows, pos_cols):
    patch_side = probe.shape[1]
    tile_rows = consensus.shape[1]
    tile_cols = consensus.shape[2]
    ext_rows = local_copy.shape[1]
    ext_cols = local_copy.shape[2]
    patch_count = pos_rows.shape[0]
    row_index = lax.axis_index("row")
    col_index = lax.axis_index("col")
    top_rows = pos_rows - row_index * tile_rows
    left_cols = pos_cols - col_index * tile_cols
    cosine, sine = dft_tables(patch_side)
    probe_re = probe[0]
    probe_im = probe[1]

    def take_window(top_row, left_col):
        return lax.dynamic_slice(
            local_copy, (top_row * 0, top_row, left_col), (2, patch_side, patch_side)
        )

    def block_step(block_index, state_pair):
        gradient, probe_grad = state_pair
        first_patch = block_index * PATCH_BLOCK
        block_tops = lax.dynamic_slice_in_dim(top_rows, first_patch, PATCH_BLOCK)
        block_lefts = lax.dynamic_slice_in_dim(left_cols, first_patch, PATCH_BLOCK)
        block_data = lax.dynamic_slice_in_dim(intensity, first_patch, PATCH_BLOCK, 0)
        patches = jax.vmap(take_window)(block_tops, block_lefts)
        object_re = patches[:, 0]
        object_im = patches[:, 1]
        wave_re = probe_re * object_re - probe_im * object_im
        wave_im = probe_re * object_im + probe_im * object_re
        spec_re, spec_im = transform(wave_re, wave_im, cosine, sine, 1.0)
        residue = spec_re * spec_re + spec_im * spec_im - block_data
        misfit_re, misfit_im = transform(residue * spec_re, residue * spec_im, cosine, sine, -1.0)
        object_grad_re = probe_re * misfit_re + probe_im * misfit_im
        object_grad_im = probe_re * misfit_im - probe_im * misfit_re
        probe_term_re = jnp.sum(object_re * misfit_re + object_im * misfit_im, axis=0)
        probe_term_im = jnp.sum(object_re * misfit_im - object_im * misfit_re, axis=0)
        for member in range(PATCH_BLOCK):
            patch_term = jnp.stack([object_grad_re[member], object_grad_im[member]])
            top_row = block_tops[member]
            left_col = block_lefts[member]
            current = lax.dynamic_slice(
                gradient, (top_row * 0, top_row, left_col), (2, patch_side, patch_side)
            )
            gradient = lax.dynamic_update_slice(
                gradient, current + patch_term, (top_row * 0, top_row, left_col)
            )
        return (gradient, probe_grad + jnp.stack([probe_term_re, probe_term_im]))

    start_grad = jnp.zeros((2, ext_rows, ext_cols), jnp.float32)
    start_probe = jnp.zeros((2, patch_side, patch_side), jnp.float32)
    gradient, probe_grad = lax.fori_loop(
        0, patch_count // PATCH_BLOCK, block_step, (start_grad, start_probe)
    )
    local_norm = jnp.sum(gradient * gradient)
    devices = lax.axis_size("row") * lax.axis_size("col")
    probe_total, norm_total = lax.psum((probe_grad, local_norm), ("row", "col"))
    probe_rms = jnp.sqrt(jnp.sum(probe_total * probe_total) / (patch_side * patch_side) + epsilon)
    new_probe = probe - probe_step * probe_total / probe_rms
    grad_scale = 1.0 / jnp.sqrt(norm_total / (devices * ext_rows * ext_cols) + epsilon)

    def extend(field):
        below = passed_along(field[:, :patch_side, :], "row", -1)
        tall = jnp.concatenate([field, below], axis=1)
        beside = passed_along(tall[:, :, :patch_side], "col", -1)
        return jnp.concatenate([tall, beside], axis=2)

    consensus_window = extend(consensus)
    new_copy = local_copy - object_step * (
        grad_scale * gradient + penalty * (local_copy - consensus_window + dual)
    )
    merged = new_copy + dual
    lower = passed_along(merged[:, tile_rows:, :], "row", 1)
    upper_part = merged[:, :tile_rows, :]
    upper_part = jnp.concatenate(
        [upper_part[:, :patch_side, :] + lower, upper_part[:, patch_side:, :]], axis=1
    )
    margin = passed_along(upper_part[:, :, tile_cols:], "col", 1)
    core_part = upper_part[:, :, :tile_cols]
    summed = jnp.concatenate(
        [core_part[:, :, :patch_side] + margin, core_part[:, :, patch_side:]], axis=2
    )
    row_cover = 1.0 + ((jnp.arange(tile_rows) < patch_side) & (row_index > 0)).astype(jnp.float32)
    col_cover = 1.0 + ((jnp.arange(tile_cols) < patch_side) & (col_index > 0)).astype(jnp.float32)
    new_consensus = summed / (row_cover[:, None] * col_cover[None, :])[None]
    new_dual = dual + new_copy - extend(new_consensus)
    return (new_copy, new_consensus, new_dual, new_probe)


def solution(mesh):
    return jax.shard_map(
        per_device,
        mesh=mesh,
        in_specs=(
            P(None, "row", "col"),
            P(None, "row", "col"),
            P(None, "row", "col"),
            P(),
            P(("row", "col"), None, None),
            P(("row", "col")),
            P(("row", "col")),
        ),
        out_specs=(P(None, "row", "col"), P(None, "row", "col"), P(None, "row", "col"), P()),
        check_vma=False,
    )
```

profile of v0, /device:TPU:33, one launch (start us, length us, event | category | flops | bytes accessed | tf_op | source)
XLA Modules:
  0.0 827.6 jit_solution(4655162079540456584)
XLA Ops:
  8.2 2.6 collective-permute-start
  13.2 5.2 collective-permute-done
  19.4 8.5 %collective-permute-start.1 = (f32[2,640,128]{2,1,0:T(8,128)}, f32[2,640,128]{2,1,0:T(8,128)}, u32[]{:S(2)}, u32[]{:S(2)}) collective-permute-start(f32[2,640,128]{2,1,0:T(8,128)} %slice.239), channel_id=1, source_target_pairs={{1,0},{2,1},{3,2},{4,3},{5,4},{6,5},{7,6},{8,7},{9,8},{10,9},{11,1... | collective-permute-start | bytes 1966088 | tf_op jit(solution)/shard_map/ppermute | solution.py:20
  28.0 418.1 %while.22 = (s32[]{:T(128)}, f32[2,640,384]{1,2,0:T(8,128)S(1)}, f32[2,128,128]{1,2,0:T(8,128)S(1)}, s32[32]{0:T(128)S(1)}, s32[32]{0:T(128)S(1)}, /*index=5*/f3...) while((s32[]{:T(128)}, f32[2,640,384]{1,2,0:T(8,128)S(1)}, ...), condition=%wide.region_3.4_spmd.clone.clone, body=%wide.region_0.3_spmd.clone.clone.sunk | while | flops 1618673664 | bytes 21365800 | solution.py:99
  45.6 12.5 %while.23 = (s32[]{:T(128)}, f32[2,640,384]{2,1,0:T(8,128)}, s32[4,3]{1,0:T(4,128)S(1)}, f32[4,2,128,128]{2,3,0,1:T(8,128)S(1)}, s32[]{:T(128)}) while((s32[]{:T(128)}, f32[2,640,384]{2,1,0:T(8,128)}, s32[4,3]{1,0:T(4,128)S(1)}, f32[4,2,128,128]{2,3,0,1:T(8,128)S(1)}, s32[]{:T(128)}) %tuple.98), condition=%wide.while_cond, body=%wide.while_body.sunk | while | flops 2 | bytes 786557 | solution.py:63
  46.3 2.3 dynamic-slice_bitcast_fusion.2
  75.0 2.5 dynamic_update_slice.42
  77.7 2.5 dynamic_update_slice.43
  97.8 12.5 %while.23 = (s32[]{:T(128)}, f32[2,640,384]{2,1,0:T(8,128)}, s32[4,3]{1,0:T(4,128)S(1)}, f32[4,2,128,128]{2,3,0,1:T(8,128)S(1)}, s32[]{:T(128)}) while((s32[]{:T(128)}, f32[2,640,384]{2,1,0:T(8,128)}, s32[4,3]{1,0:T(4,128)S(1)}, f32[4,2,128,128]{2,3,0,1:T(8,128)S(1)}, s32[]{:T(128)}) %tuple.98), condition=%wide.while_cond, body=%wide.while_body.sunk | while | flops 2 | bytes 786557 | solution.py:63
  98.5 2.3 dynamic-slice_bitcast_fusion.2
  104.7 2.3 dynamic-slice_bitcast_fusion.2
  122.6 2.5 dynamic_update_slice.40
  125.2 2.5 dynamic_update_slice.41
  127.8 2.4 dynamic_update_slice.42
  130.3 2.4 dynamic_update_slice.43
  150.4 12.5 %while.23 = (s32[]{:T(128)}, f32[2,640,384]{2,1,0:T(8,128)}, s32[4,3]{1,0:T(4,128)S(1)}, f32[4,2,128,128]{2,3,0,1:T(8,128)S(1)}, s32[]{:T(128)}) while((s32[]{:T(128)}, f32[2,640,384]{2,1,0:T(8,128)}, s32[4,3]{1,0:T(4,128)S(1)}, f32[4,2,128,128]{2,3,0,1:T(8,128)S(1)}, s32[]{:T(128)}) %tuple.98), condition=%wide.while_cond, body=%wide.while_body.sunk | while | flops 2 | bytes 786557 | solution.py:63
  180.9 2.5 dynamic_update_slice.43
  201.0 12.5 %while.23 = (s32[]{:T(128)}, f32[2,640,384]{2,1,0:T(8,128)}, s32[4,3]{1,0:T(4,128)S(1)}, f32[4,2,128,128]{2,3,0,1:T(8,128)S(1)}, s32[]{:T(128)}) while((s32[]{:T(128)}, f32[2,640,384]{2,1,0:T(8,128)}, s32[4,3]{1,0:T(4,128)S(1)}, f32[4,2,128,128]{2,3,0,1:T(8,128)S(1)}, s32[]{:T(128)}) %tuple.98), condition=%wide.while_cond, body=%wide.while_body.sunk | while | flops 2 | bytes 786557 | solution.py:63
  225.8 2.4 dynamic_update_slice.40
  230.8 2.5 dynamic_update_slice.42
  233.4 2.5 dynamic_update_slice.43
  253.6 12.5 %while.23 = (s32[]{:T(128)}, f32[2,640,384]{2,1,0:T(8,128)}, s32[4,3]{1,0:T(4,128)S(1)}, f32[4,2,128,128]{2,3,0,1:T(8,128)S(1)}, s32[]{:T(128)}) while((s32[]{:T(128)}, f32[2,640,384]{2,1,0:T(8,128)}, s32[4,3]{1,0:T(4,128)S(1)}, f32[4,2,128,128]{2,3,0,1:T(8,128)S(1)}, s32[]{:T(128)}) %tuple.98), condition=%wide.while_cond, body=%wide.while_body.sunk | while | flops 2 | bytes 786557 | solution.py:63
  278.3 2.4 dynamic_update_slice.40
  280.8 2.5 dynamic_update_slice.41
  283.5 2.3 dynamic_update_slice.42
  285.9 2.5 dynamic_update_slice.43
  306.1 12.5 %while.23 = (s32[]{:T(128)}, f32[2,640,384]{2,1,0:T(8,128)}, s32[4,3]{1,0:T(4,128)S(1)}, f32[4,2,128,128]{2,3,0,1:T(8,128)S(1)}, s32[]{:T(128)}) while((s32[]{:T(128)}, f32[2,640,384]{2,1,0:T(8,128)}, s32[4,3]{1,0:T(4,128)S(1)}, f32[4,2,128,128]{2,3,0,1:T(8,128)S(1)}, s32[]{:T(128)}) %tuple.98), condition=%wide.while_cond, body=%wide.while_body.sunk | while | flops 2 | bytes 786557 | solution.py:63
  330.8 2.5 dynamic_update_slice.40
  333.4 2.4 dynamic_update_slice.41
  336.0 2.5 dynamic_update_slice.42
  338.6 2.5 dynamic_update_slice.43
  358.7 12.5 %while.23 = (s32[]{:T(128)}, f32[2,640,384]{2,1,0:T(8,128)}, s32[4,3]{1,0:T(4,128)S(1)}, f32[4,2,128,128]{2,3,0,1:T(8,128)S(1)}, s32[]{:T(128)}) while((s32[]{:T(128)}, f32[2,640,384]{2,1,0:T(8,128)}, s32[4,3]{1,0:T(4,128)S(1)}, f32[4,2,128,128]{2,3,0,1:T(8,128)S(1)}, s32[]{:T(128)}) %tuple.98), condition=%wide.while_cond, body=%wide.while_body.sunk | while | flops 2 | bytes 786557 | solution.py:63
  383.5 2.5 dynamic_update_slice.40
  386.1 2.3 dynamic_update_slice.41
  388.6 2.5 dynamic_update_slice.42
  411.1 12.5 %while.23 = (s32[]{:T(128)}, f32[2,640,384]{2,1,0:T(8,128)}, s32[4,3]{1,0:T(4,128)S(1)}, f32[4,2,128,128]{2,3,0,1:T(8,128)S(1)}, s32[]{:T(128)}) while((s32[]{:T(128)}, f32[2,640,384]{2,1,0:T(8,128)}, s32[4,3]{1,0:T(4,128)S(1)}, f32[4,2,128,128]{2,3,0,1:T(8,128)S(1)}, s32[]{:T(128)}) %tuple.98), condition=%wide.while_cond, body=%wide.while_body.sunk | while | flops 2 | bytes 786557 | solution.py:63
  435.9 2.5 dynamic_update_slice.40
  438.5 2.5 dynamic_update_slice.41
  441.1 2.5 dynamic_update_slice.42
  447.3 76.1 %psum.14 = f32[]{:T(128)} all-reduce(f32[]{:T(128)} %multiply_reduce_fusion), channel_id=1, replica_groups=mesh['row'=8,'col'=32] {'row','col'}, use_global_device_ids=true, to_apply=%region_5.6 | all-reduce | flops 1 | bytes 8 | tf_op jit(solution)/shard_map/psum | solution.py:104
  525.8 4.7 fusion.151
  530.5 4.8 collective-permute-start.2
  535.4 8.1 collective-permute-done.2
  547.2 12.3 %collective-permute-done.3 = f32[2,512,128]{2,1,0:T(8,128)} collective-permute-done((f32[2,512,128]{2,1,0:T(8,128)}, f32[2,512,128]{2,1,0:T(8,128)}, u32[]{:S(2)}, u32[]{:S(2)}) %collective-permute-start.3) | collective-permute-done | bytes 524320 | tf_op jit(solution)/shard_map/ppermute | solution.py:20
  562.9 12.4 %collective-permute-done.4 = f32[2,128,256]{2,1,0:T(8,128)S(1)} collective-permute-done((f32[2,128,256]{2,1,0:T(8,128)S(1)}, f32[2,128,256]{2,1,0:T(8,128)S(1)}, u32[]{:S(2)}, u32[]{:S(2)}) %collective-permute-start.4) | collective-permute-done | bytes 262176 | tf_op jit(solution)/shard_map/ppermute | solution.py:20
  575.3 3.0 collective-permute-start.5
  579.1 234.9 %all-reduce.2.cloned.1.call-done = f32[2,128,128]{2,1,0:T(8,128)} async-done(((f32[2,128,128]{2,1,0:T(8,128)}), f32[2,128,128]{2,1,0:T(8,128)}) %all-reduce.2.cloned.1.call-update) | async-done | bytes 131088 | tf_op jit(solution)/shard_map/psum | solution.py:104
  817.8 2.9 maximum_subtract_fusion.1
  (469 shorter events, 247.4 us)
Async XLA Ops:
  7.2 6.0 copy-start.6
  7.2 6.0 copy-start.7
  7.2 806.8 %all-reduce.2.cloned.1.call-start = ((), (), s32[]{:S(2)}) async-start(), calls=%async_computation | async-start | bytes 262144 | tf_op jit(solution)/shard_map/psum | solution.py:104
  8.2 10.2 %collective-permute-start = (f32[2,128,256]{2,1,0:T(8,128)S(1)}, f32[2,128,256]{2,1,0:T(8,128)S(1)}, u32[]{:S(2)}, u32[]{:S(2)}) collective-permute-start(f32[2,128,256]{2,1,0:T(8,128)S(1)} %slice.170), channel_id=1, source_target_pairs={{32,0},{64,32},{96,64},{128,96},{160,128},{192,160},{224,192},{33,... | collective-permute-start | bytes 786440 | tf_op jit(solution)/shard_map/ppermute | solution.py:20
  18.4 9.4 %copy-start.1 = (f32[2,640,256]{2,1,0:T(8,128)}, f32[2,640,256]{2,1,0:T(8,128)S(1)}, u32[]{:S(2)}) copy-start(f32[2,640,256]{2,1,0:T(8,128)S(1)} %constant_dynamic-update-slice_fusion.1) | copy-start | bytes 3932164
  19.4 506.4 %collective-permute-start.1 = (f32[2,640,128]{2,1,0:T(8,128)}, f32[2,640,128]{2,1,0:T(8,128)}, u32[]{:S(2)}, u32[]{:S(2)}) collective-permute-start(f32[2,640,128]{2,1,0:T(8,128)} %slice.239), channel_id=1, source_target_pairs={{1,0},{2,1},{3,2},{4,3},{5,4},{6,5},{7,6},{8,7},{9,8},{10,9},{11,1... | collective-permute-start | bytes 1966088 | tf_op jit(solution)/shard_map/ppermute | solution.py:20
  523.3 2.5 copy-start.2
  530.5 12.9 %collective-permute-start.2 = (f32[2,128,384]{2,1,0:T(8,128)S(1)}, f32[2,128,384]{2,1,0:T(8,128)S(1)}, u32[]{:S(2)}, u32[]{:S(2)}) collective-permute-start(f32[2,128,384]{2,1,0:T(8,128)S(1)} %slice.241), channel_id=1, source_target_pairs={{0,32},{32,64},{64,96},{96,128},{128,160},{160,192},{192,224},{1,3... | collective-permute-start | bytes 1179656 | tf_op jit(solution)/shard_map/ppermute | solution.py:20
  543.5 0.7 copy-start.3
  545.1 14.4 %collective-permute-start.3 = (f32[2,512,128]{2,1,0:T(8,128)}, f32[2,512,128]{2,1,0:T(8,128)}, u32[]{:S(2)}, u32[]{:S(2)}) collective-permute-start(f32[2,512,128]{2,1,0:T(8,128)} %fusion.146), channel_id=1, source_target_pairs={{0,1},{1,2},{2,3},{3,4},{4,5},{5,6},{6,7},{7,8},{8,9},{9,10},{10,1... | collective-permute-start | bytes 1572872 | tf_op jit(solution)/shard_map/ppermute | solution.py:20
  547.0 13.6 %copy-start.4 = (f32[2,128,384]{2,1,0:T(8,128)S(1)}, f32[2,128,384]{2,1,0:T(8,128)}, u32[]{:S(2)}) copy-start(f32[2,128,384]{2,1,0:T(8,128)} %copy-done.3) | copy-start | bytes 1179652
  560.8 14.5 %copy-start = (f32[2,512,256]{2,1,0:T(8,128)}, f32[2,512,256]{2,1,0:T(8,128)S(1)}, u32[]{:S(2)}) copy-start(f32[2,512,256]{2,1,0:T(8,128)S(1)} %fusion.145) | copy-start | bytes 3145732
  560.8 255.5 %copy-start.5 = (f32[2,128,128]{2,1,0:T(8,128)S(1)}, f32[2,128,128]{2,1,0:T(8,128)}, u32[]{:S(2)}) copy-start(f32[2,128,128]{2,1,0:T(8,128)} %param.12) | copy-start | bytes 393220
  560.8 14.4 %collective-permute-start.4 = (f32[2,128,256]{2,1,0:T(8,128)S(1)}, f32[2,128,256]{2,1,0:T(8,128)S(1)}, u32[]{:S(2)}, u32[]{:S(2)}) collective-permute-start(f32[2,128,256]{2,1,0:T(8,128)S(1)} %slice.247), channel_id=1, source_target_pairs={{32,0},{64,32},{96,64},{128,96},{160,128},{192,160},{224,192},{33,... | collective-permute-start | bytes 786440 | tf_op jit(solution)/shard_map/ppermute | solution.py:20
  575.3 242.5 %collective-permute-start.5 = (f32[2,640,128]{2,1,0:T(8,128)S(1)}, f32[2,640,128]{2,1,0:T(8,128)}, u32[]{:S(2)}, u32[]{:S(2)}) collective-permute-start(f32[2,640,128]{2,1,0:T(8,128)S(1)} %pad_maximum_fusion), channel_id=1, source_target_pairs={{1,0},{2,1},{3,2},{4,3},{5,4},{6,5},{7,6},{8,7},{9,8},{10,9},{11,1... | collective-permute-start | bytes 1966088 | tf_op jit(solution)/shard_map/ppermute | solution.py:20
Sparse Core Ops, SparseCore 0:
  579.2 234.7 all-reduce.1
where the time goes:
time: 833 us; the launch traced here: 828 us
  waiting for transfers between devices  273 us (33%)
  local copies, waits for them, and re-layouts  202 us (24%)
  loops' own time  123 us (15%)
  matrix products  95.3 us (11%)
  blocking collectives  76.1 us (9%)
  starting transfers between devices  22.8 us (3%)
  other arithmetic  19.2 us (2%)
  between operations  15.7 us (2%)
    psum x1, waiting for transfers between devices, per_device(): probe_total, norm_total = lax.psum((probe_grad, local_norm), ('row', 'col'))  235 us
    another operation x1, loops' own time, per_device(): lax.fori_loop(0, patch_count // PATCH_BLOCK, block_step, (start_grad, sta...  122 us
    gather x160, local copies, waits for them, and re-layouts  98.8 us
    psum x1, blocking collectives, per_device(): probe_total, norm_total = lax.psum((probe_grad, local_norm), ('row', 'col'))  76.1 us
    dynamic_update_slice x32, local copies, waits for them, and re-layouts, block_step(): lax.dynamic_update_slice(gradient, current + patch_term, (top_row * 0, to...  75.7 us
    dot_general x64, matrix products, times_right(): jnp.einsum('bij,jk->bik', values, table, precision=lax.Precision.HIGHEST)  48.8 us
    dot_general x64, matrix products, times_left(): jnp.einsum('ij,bjk->bik', table, values, precision=lax.Precision.HIGHEST)  46.5 us
    ppermute x6, waiting for transfers between devices, passed_along(): lax.ppermute(value, axis, [(source, source + steps) for source in range(f...  38 us
  transfers between devices with their start and end apart: 7, of which 5 were waited for; matrix products, arithmetic and copies ran while one was open for 37% of the time, Pallas kernels for 0%

commit v1 on v0

v1 whole, which is shorter than its diff:
```python
import functools
import math

import jax
import jax.numpy as jnp
import ml_dtypes
import numpy as np
from jax import lax
from jax.experimental import pallas as pl
from jax.experimental.pallas import tpu as pltpu
from jax.sharding import PartitionSpec as P

MESH = pl.DeviceIdType.MESH
F32 = jnp.float32
BF16 = jnp.bfloat16
SIDE = 128
BATCH = 8
FAST = 8

object_step = 0.3
penalty = 1.0
probe_step = 0.5
epsilon = 1e-06


def dft_tables():
    index = np.arange(SIDE)
    angle = 2.0 * np.pi * ((index[:, None] * index[None, :]) % SIDE) / SIDE
    cosine = np.cos(angle) / math.sqrt(SIDE)
    sine = np.sin(angle) / math.sqrt(SIDE)
    forward = np.block([[cosine, -sine], [sine, cosine]])
    backward = np.block([[cosine, sine], [-sine, cosine]])
    parts = []
    for table in (forward, backward):
        high = table.astype(ml_dtypes.bfloat16)
        parts += [high, (table - high.astype(np.float64)).astype(ml_dtypes.bfloat16)]
    return np.stack(parts)


def halves(value):
    high = value.astype(BF16)
    return high, (value - high.astype(F32)).astype(BF16)


def times_right(value, high_table, low_table):
    high, low = halves(value)
    return jnp.dot(
        jnp.concatenate([high, low, high], 1),
        jnp.concatenate([high_table, high_table, low_table], 0),
        preferred_element_type=F32,
    )


def times_left(high_table, low_table, value):
    high, low = halves(value)
    return jnp.dot(
        jnp.concatenate([high_table, low_table, high_table], 1),
        jnp.concatenate([high, high, low], 0),
        preferred_element_type=F32,
    )


def swapped(value):
    s = SIDE
    return jnp.concatenate(
        [
            jnp.concatenate([value[:s, :s], value[s:, :s]], 1),
            jnp.concatenate([value[:s, s:], value[s:, s:]], 1),
        ],
        0,
    )


def patch_body(
    rows_ref, cols_ref, copy_hbm, probe_ref, data_hbm, tables_ref,
    grad_ref, probe_grad_ref, norm_ref,
    copy_ref, data_ref, sems,
):
    s = SIDE
    count = data_ref.shape[0]
    blocks, ext_rows = copy_ref.shape[1:3]
    tile_rows, tile_cols = ext_rows - s, (blocks - 1) * s
    moves = []
    for block in range(blocks):
        moves.append(
            pltpu.make_async_copy(
                copy_hbm.at[:, :, pl.ds(block * s, s)], copy_ref.at[:, block], sems.at[block]
            )
        )
    for part in range(count // BATCH):
        span = pl.ds(part * BATCH, BATCH)
        moves.append(
            pltpu.make_async_copy(data_hbm.at[span], data_ref.at[span], sems.at[blocks + part])
        )
    for move in moves:
        move.start()
    grad_ref[...] = jnp.zeros_like(grad_ref)
    probe_grad_ref[...] = jnp.zeros_like(probe_grad_ref)
    lane = lax.broadcasted_iota(jnp.int32, (s, s), 1)
    for move in moves:
        move.wait()

    def step(index, carry):
        forward = (tables_ref[0], tables_ref[1])
        backward = (tables_ref[2], tables_ref[3])
        probe_re, probe_im = probe_ref[0], probe_ref[1]
        places, fields = [], []
        for member in range(BATCH):
            top = rows_ref[index * BATCH + member] & (tile_rows - 1)
            left = cols_ref[index * BATCH + member] & (tile_cols - 1)
            block, shift = left // s, left % s
            places.append((top, block, shift))
            field = []
            for part in range(2):
                near = copy_ref[part, block, pl.ds(top, s), :]
                far = copy_ref[part, block + 1, pl.ds(top, s), :]
                field.append(pltpu.roll(jnp.where(lane >= shift, near, far), (s - shift) % s, 1))
            fields.append(field)
        sum_re = jnp.zeros((s, s), F32)
        sum_im = jnp.zeros((s, s), F32)
        for first in range(0, BATCH, 2):
            wave = jnp.concatenate(
                [
                    jnp.concatenate(
                        [probe_re * re - probe_im * im, probe_re * im + probe_im * re], 1
                    )
                    for re, im in fields[first : first + 2]
                ],
                0,
            )
            spectrum = times_left(*backward, swapped(times_right(wave, *forward)))
            spec_re, spec_im = spectrum[:s], spectrum[s:]
            data = jnp.concatenate(
                [data_ref[index * BATCH + first], data_ref[index * BATCH + first + 1]], 1
            )
            residue = spec_re * spec_re + spec_im * spec_im - data
            weighted = jnp.concatenate([residue * spec_re, residue * spec_im], 0)
            misfit = times_right(swapped(times_left(*forward, weighted)), *backward)
            for second in range(2):
                member = first + second
                mis_re = misfit[second * s : (second + 1) * s, :s]
                mis_im = misfit[second * s : (second + 1) * s, s:]
                re, im = fields[member]
                sum_re += re * mis_re + im * mis_im
                sum_im += re * mis_im - im * mis_re
                top, block, shift = places[member]
                terms = (probe_re * mis_re + probe_im * mis_im, probe_re * mis_im - probe_im * mis_re)
                for part in range(2):
                    term = pltpu.roll(terms[part], shift, 1)
                    grad_ref[part, block, pl.ds(top, s), :] += jnp.where(lane >= shift, term, 0.0)
                    grad_ref[part, block + 1, pl.ds(top, s), :] += jnp.where(lane >= shift, 0.0, term)
        probe_grad_ref[0] += sum_re
        probe_grad_ref[1] += sum_im
        return carry

    lax.fori_loop(0, count // BATCH, step, 0)

    def squares(index, total):
        for part in range(2):
            for block in range(blocks):
                value = grad_ref[part, block, pl.ds(pl.multiple_of(index * 8, 8), 8), :]
                total = total + value * value
        return total

    norm_ref[...] = lax.fori_loop(0, ext_rows // 8, squares, jnp.zeros((8, s), F32))


def patch_gradients(pos_rows, pos_cols, local_copy, probe, intensity):
    s = SIDE
    count = intensity.shape[0]
    ext_rows, ext_cols = local_copy.shape[1:]
    blocks = ext_cols // s
    vmem, smem = pl.BlockSpec(memory_space=pltpu.VMEM), pl.BlockSpec(memory_space=pltpu.SMEM)
    hbm = pl.BlockSpec(memory_space=pl.ANY)
    return pl.pallas_call(
        patch_body,
        in_specs=[smem, smem, hbm, vmem, hbm, vmem],
        out_specs=[vmem, vmem, vmem],
        out_shape=[
            jax.ShapeDtypeStruct((2, blocks, ext_rows, s), F32),
            jax.ShapeDtypeStruct((2, s, s), F32),
            jax.ShapeDtypeStruct((8, s), F32),
        ],
        scratch_shapes=[
            pltpu.VMEM((2, blocks, ext_rows, s), F32),
            pltpu.VMEM((count, s, s), F32),
            pltpu.SemaphoreType.DMA((blocks + count // BATCH,)),
        ],
        compiler_params=pltpu.CompilerParams(vmem_limit_bytes=50 * 2**20),
        cost_estimate=pl.CostEstimate(
            flops=count * 4 * 3 * 2 * s * 256 * 256, bytes_accessed=8 * 2**20, transcendentals=0
        ),
    )(pos_rows, pos_cols, local_copy, probe, intensity, jnp.asarray(dft_tables()))


def finish_body(
    n_row, n_col, fast, slow,
    copy_hbm, dual_hbm, grad_hbm, cons_hbm, up_hbm, left_hbm, diag_hbm, probe_grad_ref, norm_ref, probe_ref,
    new_copy_hbm, new_cons_hbm, new_dual_hbm, new_probe_ref,
    copy_v, dual_v, grad_v, cons_v, w_v, new_copy_v, new_cons_v, new_dual_v,
    from_up, from_down, from_left, from_right,
    fast_out, fast_in, slow_out, slow_in, row_out, row_in, slow_all, fast_all,
    load_sems, store_sems, halo_send, halo_recv, sum_send, sum_recv,
):
    s = SIDE
    a, b = lax.axis_index("row"), lax.axis_index("col")
    low, high = b % fast, b // fast
    ext_rows, ext_cols = copy_v.shape[1:]
    tile_rows, tile_cols = cons_v.shape[1] - s, cons_v.shape[2] - s
    blocks = ext_cols // s
    last = blocks - 1

    loads = []
    for index, (source, target) in enumerate(
        [
            (copy_hbm, copy_v),
            (dual_hbm, dual_v),
            (grad_hbm, grad_v),
            (cons_hbm, cons_v.at[:, pl.ds(0, tile_rows), pl.ds(0, tile_cols)]),
            (up_hbm, cons_v.at[:, pl.ds(tile_rows, s), pl.ds(0, tile_cols)]),
            (left_hbm, cons_v.at[:, pl.ds(0, tile_rows), pl.ds(tile_cols, s)]),
            (diag_hbm, cons_v.at[:, pl.ds(tile_rows, s), pl.ds(tile_cols, s)]),
        ]
    ):
        loads.append(pltpu.make_async_copy(source, target, load_sems.at[index]))
        loads[-1].start()

    up, down = ((a + n_row - 1) % n_row, b), ((a + 1) % n_row, b)
    left, right = (a, (b + n_col - 1) % n_col), (a, (b + 1) % n_col)

    def fast_peer(index):
        return (a, high * fast + index)

    def slow_peer(index):
        return (a, index * fast + low)

    def row_peer(index):
        return (index, b)

    groups = ((fast_peer, low, fast), (slow_peer, high, slow), (row_peer, a, n_row))
    greeted = [up, down, left, right]
    for peer, mine, size in groups:
        greeted += [peer((mine + hop) % size) for hop in range(1, size)]
    barrier = pltpu.get_barrier_semaphore()
    for device in greeted:
        pl.semaphore_signal(barrier, inc=1, device_id=device, device_id_type=MESH)
    pl.semaphore_wait(barrier, len(greeted))

    sent = []

    def send(source, target, send_sem, recv_sem, device):
        move = pltpu.make_async_remote_copy(
            src_ref=source, dst_ref=target, send_sem=send_sem, recv_sem=recv_sem,
            device_id=device, device_id_type=MESH,
        )
        move.start()
        sent.append(move)

    def spread(phase, group, source_of, slots):
        peer, mine, size = group
        for hop in range(1, size):
            other = (mine + hop) % size
            send(source_of(other), slots.at[mine], sum_send.at[phase, hop], sum_recv.at[phase, hop], peer(other))

        def arrived():
            for hop in range(1, size):
                other = (mine + size - hop) % size
                pltpu.make_async_remote_copy(
                    src_ref=source_of(other), dst_ref=slots.at[other], send_sem=sum_send.at[phase, hop],
                    recv_sem=sum_recv.at[phase, hop], device_id=peer(other), device_id_type=MESH,
                ).wait_recv()

        return arrived

    def total_of(slots, size):
        total = slots[0]
        for index in range(1, size):
            total = total + slots[index]
        return total

    share, piece = fast_out.shape[1] - 8, slow_out.shape[1] - 8
    for index in range(fast):
        fast_out[index, :share] = probe_grad_ref[pl.ds(index * share, share), :]
        fast_out[index, share:] = norm_ref[...]
    arrived = spread(0, groups[0], lambda other: fast_out.at[other], fast_in)
    fast_in[low] = fast_out[low]
    arrived()
    partial = total_of(fast_in, fast)
    for index in range(slow):
        slow_out[index, :piece] = partial[index * piece : (index + 1) * piece]
        slow_out[index, piece:] = partial[share:]
    arrived = spread(1, groups[1], lambda other: slow_out.at[other], slow_in)
    slow_in[high] = slow_out[high]
    arrived()
    row_out[...] = total_of(slow_in, slow)
    arrived = spread(2, groups[2], lambda other: row_out, row_in)
    row_in[a] = row_out[...]
    arrived()
    whole = total_of(row_in, n_row)
    slow_all[high] = whole[:piece]
    slow_arrived = spread(3, groups[1], lambda other: slow_all.at[high], slow_all)

    squares = jnp.sum(whole[piece:], keepdims=True)
    scale = object_step / jnp.sqrt(squares / (n_row * n_col * ext_rows * ext_cols) + epsilon)
    for load in loads:
        load.wait()

    keep = 1.0 - object_step * penalty

    def fill(first, count, block):
        columns = pl.ds(block * s, s)
        span = pl.ds(first, count)
        for part in range(2):
            old, dual = copy_v[part, span, columns], dual_v[part, span, columns]
            w_v[part, block, span, :] = keep * (old + dual) - scale * grad_v[part, block, span, :]

    for block in range(blocks):
        fill(0, s, block)
        fill(tile_rows, s, block)
    lower, upper, middle = pl.ds(tile_rows, s), pl.ds(0, s), pl.ds(s, tile_rows - s)
    send(w_v.at[:, :, upper], from_down, halo_send.at[0], halo_recv.at[0], up)
    send(w_v.at[:, :, lower], from_up, halo_send.at[1], halo_recv.at[1], down)
    fill(s, tile_rows - s, 0)
    fill(s, tile_rows - s, last)
    send(w_v.at[:, 0, middle], from_right.at[:, middle], halo_send.at[2], halo_recv.at[2], left)
    send(w_v.at[:, last, middle], from_left.at[:, middle], halo_send.at[3], halo_recv.at[3], right)
    for block in range(1, last):
        fill(s, tile_rows - s, block)

    def received(index):
        sent[first_halo + index].wait_recv()

    first_halo = len(sent) - 4

    slow_arrived()
    fast_all[low] = jnp.concatenate([slow_all[index] for index in range(slow)], 0)
    fast_arrived = spread(4, groups[0], lambda other: fast_all.at[low], fast_all)

    has_up, has_down = (a > 0).astype(F32), (a < n_row - 1).astype(F32)
    has_left, has_right = (b > 0).astype(F32), (b < n_col - 1).astype(F32)

    received(0)
    received(1)
    for part in range(2):
        for block in range(blocks):
            from_up[part, block] = w_v[part, block, upper] + has_up * from_up[part, block]
            from_down[part, block] = w_v[part, block, lower] + has_down * from_down[part, block]
    corner = len(sent)
    send(from_up.at[:, 0], from_right.at[:, upper], halo_send.at[4], halo_recv.at[4], left)
    send(from_down.at[:, 0], from_right.at[:, lower], halo_send.at[5], halo_recv.at[5], left)
    send(from_up.at[:, last], from_left.at[:, upper], halo_send.at[6], halo_recv.at[6], right)
    send(from_down.at[:, last], from_left.at[:, lower], halo_send.at[7], halo_recv.at[7], right)

    for part in range(2):
        for block in range(blocks):
            columns = pl.ds(block * s, s)
            new_copy_v[part, :, columns] = (
                w_v[part, block] - dual_v[part, :, columns] + (object_step * penalty) * cons_v[part, :, columns]
            )
        for block in range(1, last):
            columns = pl.ds(block * s, s)
            new_cons_v[part, middle, columns] = (
                w_v[part, block, middle] + (object_step * penalty) * cons_v[part, middle, columns]
            )
            new_dual_v[part, middle, columns] = jnp.zeros((tile_rows - s, s), F32)
    stores = [pltpu.make_async_copy(new_copy_v, new_copy_hbm, store_sems.at[0])]
    stores[0].start()

    def finish(span, block, total, own, cover_rows, inside_rows):
        columns = pl.ds(block * s, s)
        for part in range(2):
            summed = total(part)
            cover = cover_rows
            inside = inside_rows
            if block == 0:
                summed = summed + has_left * from_left[part, span]
                cover = cover * (1.0 + has_left)
            if block == last:
                summed = summed + has_right * from_right[part, span]
                cover = cover * (1.0 + has_right)
                inside = inside * has_right
            mean = summed * (1.0 / cover)
            new_dual_v[part, span, columns] = own(part) - inside * mean
            if block < last and own is not None and span is not lower:
                new_cons_v[part, span, columns] = mean + (object_step * penalty) * cons_v[part, span, columns]

    one = jnp.float32(1.0)

    def own_of(block, span):
        return lambda part: w_v[part, block, span]

    for block in range(1, last):
        finish(upper, block, lambda part: from_up[part, block], own_of(block, upper), 1.0 + has_up, one)
        finish(lower, block, lambda part: from_down[part, block], own_of(block, lower), 1.0 + has_down, has_down)
    received(2)
    received(3)
    for block in (0, last):
        finish(middle, block, own_of(block, middle), own_of(block, middle), one, one)
    for index in range(4):
        sent[corner + index].wait_recv()
    for block in (0, last):
        finish(upper, block, lambda part: from_up[part, block], own_of(block, upper), 1.0 + has_up, one)
        finish(lower, block, lambda part: from_down[part, block], own_of(block, lower), 1.0 + has_down, has_down)
    stores += [
        pltpu.make_async_copy(new_cons_v, new_cons_hbm, store_sems.at[1]),
        pltpu.make_async_copy(new_dual_v, new_dual_hbm, store_sems.at[2]),
    ]
    stores[1].start()
    stores[2].start()

    fast_arrived()
    power = jnp.zeros((share, s), F32)
    for index in range(fast):
        power = power + fast_all[index] * fast_all[index]
    rate = probe_step / jnp.sqrt(jnp.sum(power, keepdims=True) / (s * s) + epsilon)
    for index in range(fast):
        span = pl.ds(index * share, share)
        new_probe_ref[span, :] = probe_ref[span, :] - rate * fast_all[index]

    for move in sent:
        move.wait_send()
    for store in stores:
        store.wait()


def finish_step(n_row, n_col, local_copy, dual, gradient, consensus, halos, probe_grad, norm, probe):
    s = SIDE
    ext_rows, ext_cols = local_copy.shape[1:]
    tile_rows, tile_cols = consensus.shape[1:]
    blocks = ext_cols // s
    fast = min(FAST, n_col)
    slow = n_col // fast
    share = 2 * s // fast
    piece = share // slow
    vmem, hbm = pl.BlockSpec(memory_space=pltpu.VMEM), pl.BlockSpec(memory_space=pl.ANY)
    big = max(fast, slow, n_row)
    return pl.pallas_call(
        functools.partial(finish_body, n_row, n_col, fast, slow),
        in_specs=[hbm] * 7 + [vmem] * 3,
        out_specs=[hbm] * 3 + [vmem],
        out_shape=[
            jax.ShapeDtypeStruct(local_copy.shape, F32),
            jax.ShapeDtypeStruct(consensus.shape, F32),
            jax.ShapeDtypeStruct(local_copy.shape, F32),
            jax.ShapeDtypeStruct((2 * s, s), F32),
        ],
        scratch_shapes=[
            pltpu.VMEM(local_copy.shape, F32),
            pltpu.VMEM(local_copy.shape, F32),
            pltpu.VMEM((2, blocks, ext_rows, s), F32),
            pltpu.VMEM(local_copy.shape, F32),
            pltpu.VMEM((2, blocks, ext_rows, s), F32),
            pltpu.VMEM(local_copy.shape, F32),
            pltpu.VMEM(consensus.shape, F32),
            pltpu.VMEM(local_copy.shape, F32),
            pltpu.VMEM((2, blocks, s, s), F32),
            pltpu.VMEM((2, blocks, s, s), F32),
            pltpu.VMEM((2, ext_rows, s), F32),
            pltpu.VMEM((2, ext_rows, s), F32),
            pltpu.VMEM((fast, share + 8, s), F32),
            pltpu.VMEM((fast, share + 8, s), F32),
            pltpu.VMEM((slow, piece + 8, s), F32),
            pltpu.VMEM((slow, piece + 8, s), F32),
            pltpu.VMEM((piece + 8, s), F32),
            pltpu.VMEM((n_row, piece + 8, s), F32),
            pltpu.VMEM((slow, piece, s), F32),
            pltpu.VMEM((fast, share, s), F32),
            pltpu.SemaphoreType.DMA((7,)),
            pltpu.SemaphoreType.DMA((3,)),
            pltpu.SemaphoreType.DMA((8,)),
            pltpu.SemaphoreType.DMA((8,)),
            pltpu.SemaphoreType.DMA((5, big)),
            pltpu.SemaphoreType.DMA((5, big)),
        ],
        compiler_params=pltpu.CompilerParams(
            collective_id=0, has_side_effects=True, vmem_limit_bytes=50 * 2**20
        ),
        cost_estimate=pl.CostEstimate(flops=10**7, bytes_accessed=16 * 2**20, transcendentals=0),
    )(
        local_copy, dual, gradient, consensus, *halos,
        probe_grad.reshape(2 * s, s), norm, probe.reshape(2 * s, s),
    )


def per_device(n_row, n_col, local_copy, dual, consensus, probe, intensity, pos_rows, pos_cols):
    s = SIDE
    over = [(i * n_col + j, i, j) for i in range(n_row) for j in range(n_col)]
    from_below = lax.ppermute(consensus[:, :s, :], "row", [(i, i - 1) for i in range(1, n_row)])
    from_right = lax.ppermute(consensus[:, :, :s], "col", [(j, j - 1) for j in range(1, n_col)])
    from_both = lax.ppermute(
        consensus[:, :s, :s], ("row", "col"),
        [(index, index - n_col - 1) for index, i, j in over if i > 0 and j > 0],
    )
    gradient, probe_grad, norm = patch_gradients(pos_rows, pos_cols, local_copy, probe, intensity)
    new_copy, new_consensus, new_dual, new_probe = finish_step(
        n_row, n_col, local_copy, dual, gradient, consensus, (from_below, from_right, from_both),
        probe_grad, norm, probe,
    )
    return new_copy, new_consensus, new_dual, new_probe.reshape(probe.shape)


def solution(mesh):
    field = P(None, "row", "col")
    both = ("row", "col")
    return jax.shard_map(
        functools.partial(per_device, mesh.shape["row"], mesh.shape["col"]),
        mesh=mesh,
        in_specs=(field, field, field, P(), P(both, None, None), P(both), P(both)),
        out_specs=(field, field, field, P()),
        check_vma=False,
    )
```

time: 833 us -> 98.6 us (0.12)
  waiting for transfers between devices: 273 us -> 0.01 us
  local copies, waits for them, and re-layouts: 202 us -> 14.3 us
  loops' own time: 123 us -> 0 us
  matrix products: 95.3 us -> 0 us
  blocking collectives: 76.1 us -> 0 us
  Pallas kernels: 0 us -> 71.7 us
  other arithmetic: 19.2 us -> 0 us
  between operations: 15.7 us -> 0.73 us
  starting transfers between devices: 22.8 us -> 11.5 us
    psum x1 -> x0, waiting for transfers between devices: 235 us -> none  [per_device(): probe_total, norm_total = lax.psum((probe_grad, local_norm), ('row', 'col'))]
    another operation x9 -> x0, loops' own time: 123 us -> none  [the longest x1 122 us: per_device(): lax.fori_loop(0, patch_count // PATCH_BLOCK, block_step, (start_grad, sta...]
    gather x160 -> x0, local copies, waits for them, and re-layouts: 98.8 us -> none
    dot_general x128 -> x0, matrix products: 95.3 us -> none  [the longest x64 48.8 us: times_right(): jnp.einsum('bij,jk->bik', values, table, precision=lax.Precision.HIGHEST)]
    psum x1 -> x0, blocking collectives: 76.1 us -> none  [per_device(): probe_total, norm_total = lax.psum((probe_grad, local_norm), ('row', 'col'))]
    dynamic_update_slice x32 -> x0, local copies, waits for them, and re-layouts: 75.7 us -> none  [block_step(): lax.dynamic_update_slice(gradient, current + patch_term, (top_row * 0, to...]
    pallas_call x0 -> x2, Pallas kernels: none -> 71.7 us  [the longest x1 51.1 us: finish_step(): pl.pallas_call(functools.partial(finish_body, n_row, n_col, fast, slow),...]
    ppermute x6 -> x3, waiting for transfers between devices: 38 us -> 0.01 us  [the longest x1 0.01 us: per_device(): lax.ppermute(consensus[:, :s, :s], ('row', 'col'), [(index, index - n_col...]
  transfers between devices with their start and end apart: 7 -> 3, of which waited for: 5 -> 0; matrix products, arithmetic and copies ran while one was open for 37% -> 2% of each run, Pallas kernels for 0% -> 21%
where the time goes in v1:
time: 98.6 us; the launch traced here: 98.2 us
  Pallas kernels  71.7 us (73%)
  local copies, waits for them, and re-layouts  14.3 us (15%)
  starting transfers between devices  11.5 us (12%)
    pallas_call x1, Pallas kernels, finish_step(): pl.pallas_call(functools.partial(finish_body, n_row, n_col, fast, slow),...  51.1 us
    pallas_call x1, Pallas kernels, patch_gradients(): pl.pallas_call(patch_body, in_specs=[smem, smem, hbm, vmem, hbm, vmem], o...  20.6 us
    unnamed x20, local copies, waits for them, and re-layouts  11.3 us
    ppermute x1, starting transfers between devices, per_device(): lax.ppermute(consensus[:, :s, :s], ('row', 'col'), [(index, index - n_col...  6.94 us
    ppermute x1, starting transfers between devices, per_device(): lax.ppermute(consensus[:, :, :s], 'col', [(j, j - 1) for j in range(1, n_...  2.59 us
  transfers between devices with their start and end apart: 3, of which 0 were waited for; matrix products, arithmetic and copies ran while one was open for 2% of the time, Pallas kernels for 21%

profile of v1, /device:TPU:33, one launch (start us, length us, event | category | flops | bytes accessed | tf_op | source)
XLA Modules:
  0.0 98.2 jit_solution(11384261841262827569)
XLA Ops:
  0.6 0.9 slice.11
  1.6 6.9 %collective-permute-start.2 = (f32[2,128,128]{2,1,0:T(8,128)S(1)}, f32[2,128,128]{2,1,0:T(8,128)S(1)}, u32[]{:S(2)}, u32[]{:S(2)}) collective-permute-start(f32[2,128,128]{2,1,0:T(8,128)S(1)} %slice.11), channel_id=1, source_target_pairs={{33,0},{34,1},{35,2},{36,3},{37,4},{38,5},{39,6},{40,7},{41,8},{42... | collective-permute-start | bytes 393224 | tf_op jit(solution)/shard_map/ppermute | solution.py:490
  8.5 1.0 slice.9
  9.5 1.9 %collective-permute-start = (f32[2,128,256]{2,1,0:T(8,128)S(1)}, f32[2,128,256]{2,1,0:T(8,128)S(1)}, u32[]{:S(2)}, u32[]{:S(2)}) collective-permute-start(f32[2,128,256]{2,1,0:T(8,128)S(1)} %slice.9), channel_id=1, source_target_pairs={{32,0},{64,32},{96,64},{128,96},{160,128},{192,160},{224,192},{33,... | collective-permute-start | bytes 786440 | tf_op jit(solution)/shard_map/ppermute | solution.py:488
  11.4 1.1 %slice.10 = f32[2,512,128]{2,1,0:T(8,128)S(1)} slice(f32[2,512,256]{2,1,0:T(8,128)} %cons_hbm.1), slice={[0:2], [0:512], [0:128]} | slice | bytes 1048576 | tf_op jit(solution)/shard_map/slice | solution.py:489
  12.5 0.0 copy-start
  12.5 2.6 %collective-permute-start.1 = (f32[2,512,128]{2,1,0:T(8,128)S(1)}, f32[2,512,128]{2,1,0:T(8,128)S(1)}, u32[]{:S(2)}, u32[]{:S(2)}) collective-permute-start(f32[2,512,128]{2,1,0:T(8,128)S(1)} %slice.10), channel_id=1, source_target_pairs={{1,0},{2,1},{3,2},{4,3},{5,4},{6,5},{7,6},{8,7},{9,8},{10,9},{11,1... | collective-permute-start | bytes 1572872 | tf_op jit(solution)/shard_map/ppermute | solution.py:489
  15.1 0.0 copy-start.2
  15.1 0.9 copy-done.2
  16.0 0.0 copy-start.4
  16.0 0.7 copy-done.4
  16.7 0.0 copy-start.5
  16.7 0.7 copy-done.5
  17.3 0.0 copy-start.6
  17.3 1.0 %copy-done.6 = bf16[4,256,256]{2,1,0:T(8,128)(2,1)S(1)} copy-done((bf16[4,256,256]{2,1,0:T(8,128)(2,1)S(1)}, bf16[4,256,256]{2,1,0:T(8,128)(2,1)}, u32[]{:S(2)}) %copy-start.6) | copy-done | bytes 524312
  18.4 0.0 copy-start.3
  18.4 20.6 %shard_map.111 = (f32[2,3,640,128]{3,2,1,0:T(8,128)S(1)}, f32[2,128,128]{2,1,0:T(8,128)S(1)}, f32[8,128]{1,0:T(8,128)S(1)}) custom-call(s32[32]{0:T(128)S(1)} %copy-done.4, s32[32]{0:T(128)S(1)} %copy-done.5, f32[2,640,384]{2,1,0:T(8,128)} %copy_hbm.3, f32[2,128,128]{2,1,0:T(8,128)S(1)} %copy-done.2, f32[32,128,128]{2,1,0:T(8,128)} %data_hbm.1, ...), custom_call_target="tpu_custom_call" | custom-call | flops 6442450944 | bytes 8388608 | tf_op jit(solution)/shard_map/pallas_call | solution.py:175
  39.0 0.0 copy-start.1
  39.0 1.3 %copy-done.1 = f32[2,3,640,128]{3,2,1,0:T(8,128)} copy-done((f32[2,3,640,128]{3,2,1,0:T(8,128)}, f32[2,3,640,128]{3,2,1,0:T(8,128)S(1)}, u32[]{:S(2)}) %copy-start.1) | copy-done | bytes 1966104
  40.2 0.0 collective-permute-done.2.diag_hbm
  40.2 0.0 collective-permute-done.up_hbm
  40.2 0.0 collective-permute-done.1.left_hbm
  40.3 0.0 copy-done
  40.3 0.0 copy-done.3
  40.3 51.1 %shard_map.112 = (f32[2,640,384]{2,1,0:T(8,128)}, f32[2,512,256]{2,1,0:T(8,128)S(1)}, f32[2,640,384]{2,1,0:T(8,128)}, f32[256,128]{1,0:T(8,128)S(1)}) custom-call(f32[2,640,384]{2,1,0:T(8,128)} %copy_hbm.3, f32[2,640,384]{2,1,0:T(8,128)} %dual_hbm.1, f32[2,3,640,128]{3,2,1,0:T(8,128)} %copy-done.1, f32[2,512,256]{2,1,0:T(8,128)S(1)} %copy-done, ...), custom_call_target="tpu_custom_call" | custom-call | flops 10000000 | bytes 16777216 | tf_op jit(solution)/shard_map/pallas_call | solution.py:437
  91.4 2.9 %copy.16 = f32[2,640,384]{2,1,0:T(8,128)} copy(f32[2,640,384]{2,1,0:T(8,128)} %get-tuple-element.22) | data formatting | bytes 3932160
  94.3 0.0 copy-start.7
  94.3 1.0 copy.17
  95.3 1.0 copy-done.7
  96.2 1.3 %copy.18 = f32[2,640,384]{2,1,0:T(8,128)} copy(f32[2,640,384]{2,1,0:T(8,128)S(1)} %copy-done.7) | data formatting | bytes 3932160
  97.5 0.7 copy.19
Async XLA Ops:
  1.6 38.7 %collective-permute-start.2 = (f32[2,128,128]{2,1,0:T(8,128)S(1)}, f32[2,128,128]{2,1,0:T(8,128)S(1)}, u32[]{:S(2)}, u32[]{:S(2)}) collective-permute-start(f32[2,128,128]{2,1,0:T(8,128)S(1)} %slice.11), channel_id=1, source_target_pairs={{33,0},{34,1},{35,2},{36,3},{37,4},{38,5},{39,6},{40,7},{41,8},{42... | collective-permute-start | bytes 393224 | tf_op jit(solution)/shard_map/ppermute | solution.py:490
  9.5 30.8 %collective-permute-start = (f32[2,128,256]{2,1,0:T(8,128)S(1)}, f32[2,128,256]{2,1,0:T(8,128)S(1)}, u32[]{:S(2)}, u32[]{:S(2)}) collective-permute-start(f32[2,128,256]{2,1,0:T(8,128)S(1)} %slice.9), channel_id=1, source_target_pairs={{32,0},{64,32},{96,64},{128,96},{160,128},{192,160},{224,192},{33,... | collective-permute-start | bytes 786440 | tf_op jit(solution)/shard_map/ppermute | solution.py:488
  12.5 27.8 %copy-start = (f32[2,512,256]{2,1,0:T(8,128)S(1)}, f32[2,512,256]{2,1,0:T(8,128)}, u32[]{:S(2)}) copy-start(f32[2,512,256]{2,1,0:T(8,128)} %cons_hbm.1) | copy-start | bytes 3145732
  12.5 27.7 %collective-permute-start.1 = (f32[2,512,128]{2,1,0:T(8,128)S(1)}, f32[2,512,128]{2,1,0:T(8,128)S(1)}, u32[]{:S(2)}, u32[]{:S(2)}) collective-permute-start(f32[2,512,128]{2,1,0:T(8,128)S(1)} %slice.10), channel_id=1, source_target_pairs={{1,0},{2,1},{3,2},{4,3},{5,4},{6,5},{7,6},{8,7},{9,8},{10,9},{11,1... | collective-permute-start | bytes 1572872 | tf_op jit(solution)/shard_map/ppermute | solution.py:489
  15.1 0.9 copy-start.2
  16.0 0.7 copy-start.4
  16.7 0.7 copy-start.5
  17.3 1.0 %copy-start.6 = (bf16[4,256,256]{2,1,0:T(8,128)(2,1)S(1)}, bf16[4,256,256]{2,1,0:T(8,128)(2,1)}, u32[]{:S(2)}) copy-start(bf16[4,256,256]{2,1,0:T(8,128)(2,1)} %constant.2.clone.tables_ref) | copy-start | bytes 1572868
  18.4 21.9 %copy-start.3 = (f32[2,128,128]{2,1,0:T(8,128)S(1)}, f32[2,128,128]{2,1,0:T(8,128)}, u32[]{:S(2)}) copy-start(f32[2,128,128]{2,1,0:T(8,128)} %probe_ref.1) | copy-start | bytes 393220
  39.0 1.3 %copy-start.1 = (f32[2,3,640,128]{3,2,1,0:T(8,128)}, f32[2,3,640,128]{3,2,1,0:T(8,128)S(1)}, u32[]{:S(2)}) copy-start(f32[2,3,640,128]{3,2,1,0:T(8,128)S(1)} %get-tuple-element.11.grad_hbm) | copy-start | bytes 5898244
  94.3 1.9 %copy-start.7 = (f32[2,640,384]{2,1,0:T(8,128)S(1)}, f32[2,640,384]{2,1,0:T(8,128)}, u32[]{:S(2)}) copy-start(f32[2,640,384]{2,1,0:T(8,128)} %get-tuple-element.24) | copy-start | bytes 5898244

commit v2 on v1

v2 whole, which is shorter than its diff:
```python
import functools
import math

import jax
import jax.numpy as jnp
import ml_dtypes
import numpy as np
from jax import lax
from jax.experimental import pallas as pl
from jax.experimental.pallas import tpu as pltpu
from jax.sharding import PartitionSpec as P

MESH = pl.DeviceIdType.MESH
F32 = jnp.float32
BF16 = jnp.bfloat16
SIDE = 128
BATCH = 8

object_step = 0.3
penalty = 1.0
probe_step = 0.5
epsilon = 1e-06


def dft_tables():
    index = np.arange(SIDE)
    angle = 2.0 * np.pi * ((index[:, None] * index[None, :]) % SIDE) / SIDE
    cosine = np.cos(angle) / math.sqrt(SIDE)
    sine = np.sin(angle) / math.sqrt(SIDE)
    forward = np.block([[cosine, -sine], [sine, cosine]])
    backward = np.block([[cosine, sine], [-sine, cosine]])
    parts = []
    for table in (forward, backward):
        high = table.astype(ml_dtypes.bfloat16)
        parts += [high, (table - high.astype(np.float64)).astype(ml_dtypes.bfloat16)]
    return np.stack(parts)


def halves(value):
    high = value.astype(BF16)
    return high, (value - high.astype(F32)).astype(BF16)


def times_right(value, high_table, low_table):
    high, low = halves(value)
    return jnp.dot(
        jnp.concatenate([high, low, high], 1),
        jnp.concatenate([high_table, high_table, low_table], 0),
        preferred_element_type=F32,
    )


def times_left(high_table, low_table, value):
    high, low = halves(value)
    return jnp.dot(
        jnp.concatenate([high_table, low_table, high_table], 1),
        jnp.concatenate([high, high, low], 0),
        preferred_element_type=F32,
    )


def swapped(value):
    s = SIDE
    return jnp.concatenate(
        [
            jnp.concatenate([value[:s, :s], value[s:, :s]], 1),
            jnp.concatenate([value[:s, s:], value[s:, s:]], 1),
        ],
        0,
    )


def patch_body(
    rows_hbm, cols_hbm, copy_hbm, probe_hbm, data_hbm, tables_hbm,
    grad_ref, probe_grad_ref, norm_ref,
    copy_ref, data_ref, rows_ref, cols_ref, probe_ref, tables_ref, sems,
):
    s = SIDE
    count = data_ref.shape[0]
    blocks, ext_rows = copy_ref.shape[1:3]
    tile_rows, tile_cols = ext_rows - s, (blocks - 1) * s
    moves = [
        pltpu.make_async_copy(rows_hbm, rows_ref, sems.at[0]),
        pltpu.make_async_copy(cols_hbm, cols_ref, sems.at[1]),
        pltpu.make_async_copy(probe_hbm, probe_ref, sems.at[2]),
        pltpu.make_async_copy(tables_hbm, tables_ref, sems.at[3]),
    ]
    for block in range(blocks):
        moves.append(
            pltpu.make_async_copy(
                copy_hbm.at[:, :, pl.ds(block * s, s)], copy_ref.at[:, block], sems.at[4 + block]
            )
        )
    for move in moves:
        move.start()

    def data_move(part):
        span = pl.ds(part * BATCH, BATCH)
        return pltpu.make_async_copy(data_hbm.at[span], data_ref.at[span], sems.at[4 + blocks + part])

    for part in range(count // BATCH):
        data_move(part).start()
    grad_ref[...] = jnp.zeros_like(grad_ref)
    probe_grad_ref[...] = jnp.zeros_like(probe_grad_ref)
    lane = lax.broadcasted_iota(jnp.int32, (s, s), 1)
    for move in moves:
        move.wait()

    def step(index, carry):
        data_move(index).wait()
        forward = (tables_ref[0], tables_ref[1])
        backward = (tables_ref[2], tables_ref[3])
        probe_re, probe_im = probe_ref[0], probe_ref[1]
        places, fields = [], []
        for member in range(BATCH):
            top = rows_ref[index * BATCH + member] & (tile_rows - 1)
            left = cols_ref[index * BATCH + member] & (tile_cols - 1)
            block, shift = left // s, left % s
            places.append((top, block, shift))
            field = []
            for part in range(2):
                near = copy_ref[part, block, pl.ds(top, s), :]
                far = copy_ref[part, block + 1, pl.ds(top, s), :]
                field.append(pltpu.roll(jnp.where(lane >= shift, near, far), (s - shift) % s, 1))
            fields.append(field)
        sum_re = jnp.zeros((s, s), F32)
        sum_im = jnp.zeros((s, s), F32)
        waves = []
        for first in range(0, BATCH, 2):
            wave = jnp.concatenate(
                [
                    jnp.concatenate(
                        [probe_re * re - probe_im * im, probe_re * im + probe_im * re], 1
                    )
                    for re, im in fields[first : first + 2]
                ],
                0,
            )
            waves.append(wave)
        rows_done = times_right(jnp.concatenate(waves, 0), *forward)
        misfits = []
        for first in range(0, BATCH, 2):
            spectrum = times_left(*backward, swapped(rows_done[first * s : (first + 2) * s]))
            spec_re, spec_im = spectrum[:s], spectrum[s:]
            data = jnp.concatenate(
                [data_ref[index * BATCH + first], data_ref[index * BATCH + first + 1]], 1
            )
            residue = spec_re * spec_re + spec_im * spec_im - data
            weighted = jnp.concatenate([residue * spec_re, residue * spec_im], 0)
            misfits.append(swapped(times_left(*forward, weighted)))
        misfit_all = times_right(jnp.concatenate(misfits, 0), *backward)
        for first in range(0, BATCH, 2):
            misfit = misfit_all[first * s : (first + 2) * s]
            for second in range(2):
                member = first + second
                mis_re = misfit[second * s : (second + 1) * s, :s]
                mis_im = misfit[second * s : (second + 1) * s, s:]
                re, im = fields[member]
                sum_re += re * mis_re + im * mis_im
                sum_im += re * mis_im - im * mis_re
                top, block, shift = places[member]
                terms = (probe_re * mis_re + probe_im * mis_im, probe_re * mis_im - probe_im * mis_re)
                for part in range(2):
                    term = pltpu.roll(terms[part], shift, 1)
                    grad_ref[part, block, pl.ds(top, s), :] += jnp.where(lane >= shift, term, 0.0)
                    grad_ref[part, block + 1, pl.ds(top, s), :] += jnp.where(lane >= shift, 0.0, term)
        probe_grad_ref[0] += sum_re
        probe_grad_ref[1] += sum_im
        return carry

    lax.fori_loop(0, count // BATCH, step, 0)

    def squares(index, total):
        for part in range(2):
            for block in range(blocks):
                value = grad_ref[part, block, pl.ds(pl.multiple_of(index * 8, 8), 8), :]
                total = total + value * value
        return total

    norm_ref[...] = lax.fori_loop(0, ext_rows // 8, squares, jnp.zeros((8, s), F32))


def patch_gradients(pos_rows, pos_cols, local_copy, probe, intensity):
    s = SIDE
    count = intensity.shape[0]
    ext_rows, ext_cols = local_copy.shape[1:]
    blocks = ext_cols // s
    vmem, hbm = pl.BlockSpec(memory_space=pltpu.VMEM), pl.BlockSpec(memory_space=pl.ANY)
    return pl.pallas_call(
        patch_body,
        in_specs=[hbm] * 6,
        out_specs=[vmem, vmem, vmem],
        out_shape=[
            jax.ShapeDtypeStruct((2, blocks, ext_rows, s), F32),
            jax.ShapeDtypeStruct((2, s, s), F32),
            jax.ShapeDtypeStruct((8, s), F32),
        ],
        scratch_shapes=[
            pltpu.VMEM((2, blocks, ext_rows, s), F32),
            pltpu.VMEM((count, s, s), F32),
            pltpu.SMEM(pos_rows.shape, jnp.int32),
            pltpu.SMEM(pos_cols.shape, jnp.int32),
            pltpu.VMEM(probe.shape, F32),
            pltpu.VMEM((4, 2 * s, 2 * s), BF16),
            pltpu.SemaphoreType.DMA((4 + blocks + count // BATCH,)),
        ],
        compiler_params=pltpu.CompilerParams(vmem_limit_bytes=50 * 2**20),
        cost_estimate=pl.CostEstimate(
            flops=count * 4 * 3 * 2 * s * 256 * 256, bytes_accessed=8 * 2**20, transcendentals=0
        ),
    )(pos_rows, pos_cols, local_copy, probe, intensity, jnp.asarray(dft_tables()))


def finish_body(
    n_row, n_col,
    copy_hbm, dual_hbm, grad_hbm, cons_hbm, left_hbm, probe_grad_ref, norm_ref, probe_ref,
    new_copy_ref, new_cons_ref, new_dual_ref, new_probe_ref,
    copy_v, dual_v, grad_v, cons_v, w_v,
    from_up, from_down, from_left, from_right,
    col_out, col_in, row_out, row_in, col_all,
    load_sems, halo_send, halo_recv, sum_send, sum_recv,
):
    s = SIDE
    a, b = lax.axis_index("row"), lax.axis_index("col")
    ext_rows, ext_cols = copy_v.shape[1:]
    tile_rows, tile_cols = ext_rows - s, ext_cols - s
    blocks = ext_cols // s
    last = blocks - 1
    lower, upper, middle = pl.ds(tile_rows, s), pl.ds(0, s), pl.ds(s, tile_rows - s)

    loads = []
    for index, (source, target) in enumerate(
        [
            (cons_hbm, cons_v.at[:, pl.ds(0, tile_rows), pl.ds(0, tile_cols)]),
            (left_hbm, cons_v.at[:, pl.ds(0, tile_rows), pl.ds(tile_cols, s)]),
            (copy_hbm, copy_v),
            (dual_hbm, dual_v),
            (grad_hbm, grad_v),
        ]
    ):
        loads.append(pltpu.make_async_copy(source, target, load_sems.at[index]))
        loads[-1].start()

    def row_peer(index):
        return (index, b)

    def col_peer(index):
        return (a, index)

    barrier = pltpu.get_barrier_semaphore()
    for peer, mine, size in ((row_peer, a, n_row), (col_peer, b, n_col)):

        def greet(hop, carry):
            pl.semaphore_signal(
                barrier, inc=1, device_id=peer(lax.rem(mine + hop, size)), device_id_type=MESH
            )
            return carry

        lax.fori_loop(1, size, greet, 0)
    pl.semaphore_wait(barrier, n_row + n_col - 2)

    def remote(source, target, send_sem, recv_sem, device):
        return pltpu.make_async_remote_copy(
            src_ref=source, dst_ref=target, send_sem=send_sem, recv_sem=recv_sem,
            device_id=device, device_id_type=MESH,
        )

    class Spread:
        def __init__(self, phase, peer, mine, size, source_of, slots):
            self.size = size

            def move(hop, other):
                return remote(
                    source_of(other), slots.at[mine], sum_send.at[phase, hop], sum_recv.at[phase, hop], peer(other)
                )

            def start(hop, carry):
                move(hop, lax.rem(mine + hop, size)).start()
                return carry

            def arrive(hop, carry):
                other = lax.rem(mine + size - hop, size)
                remote(
                    source_of(other), slots.at[other], sum_send.at[phase, hop], sum_recv.at[phase, hop], peer(other)
                ).wait_recv()
                return carry

            def leave(hop, carry):
                move(hop, lax.rem(mine + hop, size)).wait_send()
                return carry

            lax.fori_loop(1, size, start, 0)
            self.arrived = lambda: lax.fori_loop(1, size, arrive, 0)
            self.left = lambda: lax.fori_loop(1, size, leave, 0)

    class Halo:
        def __init__(self, index, source, target, sends, device, receives):
            move = remote(source, target, halo_send.at[index], halo_recv.at[index], device)
            self.move, self.sends, self.receives = move, sends, receives

        def start(self):
            pl.when(self.sends)(lambda: self.move.start())

        def arrived(self):
            pl.when(self.receives)(lambda: self.move.wait_recv())

        def left(self):
            pl.when(self.sends)(lambda: self.move.wait_send())

    up, down, left, right = (a - 1, b), (a + 1, b), (a, b - 1), (a, b + 1)
    is_up, is_down, is_left, is_right = a > 0, a < n_row - 1, b > 0, b < n_col - 1
    has_up, has_down = is_up.astype(F32), is_down.astype(F32)
    has_left, has_right = is_left.astype(F32), is_right.astype(F32)

    piece = col_out.shape[1] - 8
    for index in range(n_col):
        col_out[index, :piece] = probe_grad_ref[pl.ds(index * piece, piece), :]
        col_out[index, piece:] = norm_ref[...]
    first_sum = Spread(0, col_peer, b, n_col, lambda other: col_out.at[other], col_in)
    col_in[b] = col_out[b]

    cons_up = Halo(0, cons_v.at[:, upper], cons_v.at[:, lower], is_up, up, is_down)
    loads[0].wait()
    loads[1].wait()
    cons_up.start()
    pl.when(jnp.logical_not(is_down))(
        lambda: cons_v.__setitem__((slice(None), lower), jnp.zeros((2, s, ext_cols), F32))
    )

    first_sum.arrived()

    def total_of(slots, size):
        total = slots[0]
        for index in range(1, size):
            total = total + slots[index]
        return total

    row_out[...] = total_of(col_in, n_col)
    second_sum = Spread(1, row_peer, a, n_row, lambda other: row_out, row_in)
    row_in[a] = row_out[...]
    for load in loads[2:]:
        load.wait()
    second_sum.arrived()
    whole = total_of(row_in, n_row)
    squares = jnp.sum(whole[piece:], keepdims=True)
    scale = object_step / jnp.sqrt(squares / (n_row * n_col * ext_rows * ext_cols) + epsilon)
    keep = 1.0 - object_step * penalty
    pull = object_step * penalty

    def fill(first, count, block):
        columns = pl.ds(block * s, s)
        span = pl.ds(first, count)
        for part in range(2):
            old, dual = copy_v[part, span, columns], dual_v[part, span, columns]
            w_v[part, block, span, :] = keep * (old + dual) - scale * grad_v[part, block, span, :]

    rows_up = Halo(1, w_v.at[:, :, upper], from_down, is_up, up, is_down)
    rows_down = Halo(2, w_v.at[:, :, lower], from_up, is_down, down, is_up)
    mid_left = Halo(3, w_v.at[:, 0, middle], from_right.at[:, middle], is_left, left, is_right)
    mid_right = Halo(4, w_v.at[:, last, middle], from_left.at[:, middle], is_right, right, is_left)
    corners = [
        Halo(5, from_up.at[:, 0], from_right.at[:, upper], is_left, left, is_right),
        Halo(6, from_down.at[:, 0], from_right.at[:, lower], is_left, left, is_right),
        Halo(7, from_up.at[:, last], from_left.at[:, upper], is_right, right, is_left),
        Halo(8, from_down.at[:, last], from_left.at[:, lower], is_right, right, is_left),
    ]
    for block in range(blocks):
        fill(0, s, block)
    rows_up.start()
    for block in range(blocks):
        fill(tile_rows, s, block)
    rows_down.start()
    fill(s, tile_rows - s, 0)
    mid_left.start()
    fill(s, tile_rows - s, last)
    mid_right.start()
    for block in range(1, last):
        fill(s, tile_rows - s, block)

    col_all[b] = whole[:piece]
    third_sum = Spread(2, col_peer, b, n_col, lambda other: col_all.at[b], col_all)

    cons_up.arrived()
    for part in range(2):
        for block in range(blocks):
            columns = pl.ds(block * s, s)
            new_copy_ref[part, :, columns] = (
                w_v[part, block] - dual_v[part, :, columns] + pull * cons_v[part, :, columns]
            )
        for block in range(1, last):
            columns = pl.ds(block * s, s)
            new_cons_ref[part, middle, columns] = w_v[part, block, middle] + pull * cons_v[part, middle, columns]
            new_dual_ref[part, middle, columns] = jnp.zeros((tile_rows - s, s), F32)

    def neighbour(present, value):
        return jnp.where(present, value, 0.0)

    rows_up.arrived()
    rows_down.arrived()
    for part in range(2):
        for block in range(blocks):
            from_up[part, block] = w_v[part, block, upper] + neighbour(is_up, from_up[part, block])
            from_down[part, block] = w_v[part, block, lower] + neighbour(is_down, from_down[part, block])
    for corner in corners:
        corner.start()

    def finish(span, block, total, cover_rows, inside_rows):
        columns = pl.ds(block * s, s)
        for part in range(2):
            summed = total(part)
            cover = cover_rows
            inside = inside_rows
            if block == 0:
                summed = summed + neighbour(is_left, from_left[part, span])
                cover = cover * (1.0 + has_left)
            if block == last:
                summed = summed + neighbour(is_right, from_right[part, span])
                cover = cover * (1.0 + has_right)
                inside = inside * has_right
            mean = summed * (1.0 / cover)
            new_dual_ref[part, span, columns] = w_v[part, block, span] - inside * mean
            if block < last and span is not lower:
                new_cons_ref[part, span, columns] = mean + pull * cons_v[part, span, columns]

    one = jnp.float32(1.0)

    def top_and_bottom(block):
        finish(upper, block, lambda part: from_up[part, block], 1.0 + has_up, one)
        finish(lower, block, lambda part: from_down[part, block], 1.0 + has_down, has_down)

    for block in range(1, last):
        top_and_bottom(block)
    mid_left.arrived()
    mid_right.arrived()
    for block in (0, last):
        finish(middle, block, lambda part: w_v[part, block, middle], one, one)

    third_sum.arrived()
    power = jnp.zeros((piece, s), F32)
    for index in range(n_col):
        power = power + col_all[index] * col_all[index]
    rate = probe_step / jnp.sqrt(jnp.sum(power, keepdims=True) / (s * s) + epsilon)
    for index in range(n_col):
        span = pl.ds(index * piece, piece)
        new_probe_ref[span, :] = probe_ref[span, :] - rate * col_all[index]

    for corner in corners:
        corner.arrived()
    for block in (0, last):
        top_and_bottom(block)

    for move in [cons_up, rows_up, rows_down, mid_left, mid_right] + corners + [first_sum, second_sum, third_sum]:
        move.left()


def finish_step(n_row, n_col, local_copy, dual, gradient, consensus, beside, probe_grad, norm, probe):
    s = SIDE
    ext_rows, ext_cols = local_copy.shape[1:]
    blocks = ext_cols // s
    piece = 2 * s // n_col
    vmem, hbm = pl.BlockSpec(memory_space=pltpu.VMEM), pl.BlockSpec(memory_space=pl.ANY)
    return pl.pallas_call(
        functools.partial(finish_body, n_row, n_col),
        in_specs=[hbm] * 5 + [vmem] * 3,
        out_specs=[vmem] * 4,
        out_shape=[
            jax.ShapeDtypeStruct(local_copy.shape, F32),
            jax.ShapeDtypeStruct(consensus.shape, F32),
            jax.ShapeDtypeStruct(local_copy.shape, F32),
            jax.ShapeDtypeStruct((2 * s, s), F32),
        ],
        scratch_shapes=[
            pltpu.VMEM(local_copy.shape, F32),
            pltpu.VMEM(local_copy.shape, F32),
            pltpu.VMEM((2, blocks, ext_rows, s), F32),
            pltpu.VMEM(local_copy.shape, F32),
            pltpu.VMEM((2, blocks, ext_rows, s), F32),
            pltpu.VMEM((2, blocks, s, s), F32),
            pltpu.VMEM((2, blocks, s, s), F32),
            pltpu.VMEM((2, ext_rows, s), F32),
            pltpu.VMEM((2, ext_rows, s), F32),
            pltpu.VMEM((n_col, piece + 8, s), F32),
            pltpu.VMEM((n_col, piece + 8, s), F32),
            pltpu.VMEM((piece + 8, s), F32),
            pltpu.VMEM((n_row, piece + 8, s), F32),
            pltpu.VMEM((n_col, piece, s), F32),
            pltpu.SemaphoreType.DMA((5,)),
            pltpu.SemaphoreType.DMA((9,)),
            pltpu.SemaphoreType.DMA((9,)),
            pltpu.SemaphoreType.DMA((3, max(n_row, n_col))),
            pltpu.SemaphoreType.DMA((3, max(n_row, n_col))),
        ],
        compiler_params=pltpu.CompilerParams(
            collective_id=0, has_side_effects=True, vmem_limit_bytes=32 * 2**20
        ),
        cost_estimate=pl.CostEstimate(flops=10**7, bytes_accessed=16 * 2**20, transcendentals=0),
    )(
        local_copy, dual, gradient, consensus, beside,
        probe_grad.reshape(2 * s, s), norm, probe.reshape(2 * s, s),
    )


def store_body(*refs):
    count = len(refs) // 2
    sources, targets, sems = refs[:count], refs[count : 2 * count], refs[2 * count]
    moves = [
        pltpu.make_async_copy(source.at[part], target.at[part], sems.at[index, part])
        for index, (source, target) in enumerate(zip(sources, targets))
        for part in range(2)
    ]
    for move in moves:
        move.start()
    for move in moves:
        move.wait()


def store(*arrays):
    return pl.pallas_call(
        store_body,
        in_specs=[pl.BlockSpec(memory_space=pltpu.VMEM)] * len(arrays),
        out_specs=[pl.BlockSpec(memory_space=pl.ANY)] * len(arrays),
        out_shape=[jax.ShapeDtypeStruct(array.shape, F32) for array in arrays],
        scratch_shapes=[pltpu.SemaphoreType.DMA((len(arrays), 2))],
        compiler_params=pltpu.CompilerParams(vmem_limit_bytes=16 * 2**20),
    )(*arrays)


def per_device(n_row, n_col, local_copy, dual, consensus, probe, intensity, pos_rows, pos_cols):
    s = SIDE
    beside = lax.ppermute(consensus[:, :, :s], "col", [(j, j - 1) for j in range(1, n_col)])
    gradient, probe_grad, norm = patch_gradients(pos_rows, pos_cols, local_copy, probe, intensity)
    new_copy, new_consensus, new_dual, new_probe = finish_step(
        n_row, n_col, local_copy, dual, gradient, consensus, beside, probe_grad, norm, probe
    )
    return tuple(store(new_copy, new_consensus, new_dual, new_probe.reshape(probe.shape)))


def solution(mesh):
    field = P(None, "row", "col")
    both = ("row", "col")
    return jax.shard_map(
        functools.partial(per_device, mesh.shape["row"], mesh.shape["col"]),
        mesh=mesh,
        in_specs=(field, field, field, P(), P(both, None, None), P(both), P(both)),
        out_specs=(field, field, field, P()),
        check_vma=False,
    )
```

time: 98.6 us -> 79.9 us (0.81)
  local copies, waits for them, and re-layouts: 14.3 us -> 4.35 us
  starting transfers between devices: 11.5 us -> 6.65 us
  Pallas kernels: 71.7 us -> 67.9 us
    ppermute x2 -> x0, starting transfers between devices: 8.86 us -> none  [the longest x1 6.94 us: per_device(): lax.ppermute(consensus[:, :s, :s], ('row', 'col'), [(index, index - n_col...]
    unnamed x20 -> x14, local copies, waits for them, and re-layouts: 11.3 us -> 3.27 us
    ppermute x1, starting transfers between devices: 2.59 us -> 6.65 us  [per_device(): lax.ppermute(consensus[:, :, :s], 'col', [(j, j - 1) for j in range(1, n_...]
    pallas_call x2 -> x3, Pallas kernels: 71.7 us -> 67.9 us  [the longest x1 50.3 us: finish_step(): pl.pallas_call(functools.partial(finish_body, n_row, n_col), in_specs=[hb...]
    slice x2 -> x0, local copies, waits for them, and re-layouts: 1.9 us -> none  [the longest x1 0.97 us: per_device(): consensus[:, :s, :]]
  transfers between devices with their start and end apart: 3 -> 1, of which waited for: 0 -> 0; matrix products, arithmetic and copies ran while one was open for 2% -> 0% of each run, Pallas kernels for 21% -> 19%
where the time goes in v2:
time: 79.9 us; the launch traced here: 79.6 us
  Pallas kernels  67.9 us (85%)
  starting transfers between devices  6.65 us (8%)
  local copies, waits for them, and re-layouts  4.35 us (5%)
    pallas_call x1, Pallas kernels, finish_step(): pl.pallas_call(functools.partial(finish_body, n_row, n_col), in_specs=[hb...  50.3 us
    pallas_call x1, Pallas kernels, patch_gradients(): pl.pallas_call(patch_body, in_specs=[hbm] * 6, out_specs=[vmem, vmem, vme...  15.2 us
    ppermute x1, starting transfers between devices, per_device(): lax.ppermute(consensus[:, :, :s], 'col', [(j, j - 1) for j in range(1, n_...  6.65 us
    unnamed x14, local copies, waits for them, and re-layouts  3.27 us
    pallas_call x1, Pallas kernels, store(): pl.pallas_call(store_body, in_specs=[pl.BlockSpec(memory_space=pltpu.VMEM...  2.36 us
  transfers between devices with their start and end apart: 1, of which 0 were waited for; matrix products, arithmetic and copies ran while one was open for 0% of the time, Pallas kernels for 19%

profile of v2, /device:TPU:33, one launch (start us, length us, event | category | flops | bytes accessed | tf_op | source)
XLA Modules:
  0.0 79.6 jit_solution(8244533052834439344)
XLA Ops:
  0.6 1.1 %slice.3 = f32[2,512,128]{2,1,0:T(8,128)S(1)} slice(f32[2,512,256]{2,1,0:T(8,128)} %cons_hbm.1), slice={[0:2], [0:512], [0:128]} | slice | bytes 1048576 | tf_op jit(solution)/shard_map/slice | solution.py:530
  1.7 0.0 copy-start
  1.7 0.0 copy-start.1
  1.7 0.0 copy-start.2
  1.7 6.6 %collective-permute-start = (f32[2,512,128]{2,1,0:T(8,128)S(1)}, f32[2,512,128]{2,1,0:T(8,128)S(1)}, u32[]{:S(2)}, u32[]{:S(2)}) collective-permute-start(f32[2,512,128]{2,1,0:T(8,128)S(1)} %slice.3), channel_id=1, source_target_pairs={{1,0},{2,1},{3,2},{4,3},{5,4},{6,5},{7,6},{8,7},{9,8},{10,9},{11,1... | collective-permute-start | bytes 1572872 | tf_op jit(solution)/shard_map/ppermute | solution.py:530
  8.4 0.0 copy-start.3
  8.4 0.9 %copy-done.3 = f32[2,128,128]{2,1,0:T(8,128)S(1)} copy-done((f32[2,128,128]{2,1,0:T(8,128)S(1)}, f32[2,128,128]{2,1,0:T(8,128)}, u32[]{:S(2)}) %copy-start.3) | copy-done | bytes 131096
  9.3 0.0 copy-start.4
  9.3 0.7 copy-done.4
  10.0 0.0 copy-start.5
  10.0 0.7 copy-done.5
  10.6 0.0 copy-start.6
  10.6 1.0 %copy-done.6 = bf16[4,256,256]{2,1,0:T(8,128)(2,1)S(1)} copy-done((bf16[4,256,256]{2,1,0:T(8,128)(2,1)S(1)}, bf16[4,256,256]{2,1,0:T(8,128)(2,1)}, u32[]{:S(2)}) %copy-start.6) | copy-done | bytes 524312
  11.7 15.2 %shard_map.111 = (f32[2,3,640,128]{3,2,1,0:T(8,128)S(1)}, f32[2,128,128]{2,1,0:T(8,128)S(1)}, f32[8,128]{1,0:T(8,128)S(1)}) custom-call(s32[32]{0:T(128)S(1)} %copy-done.4, s32[32]{0:T(128)S(1)} %copy-done.5, f32[2,640,384]{2,1,0:T(8,128)} %copy_hbm.3, f32[2,128,128]{2,1,0:T(8,128)S(1)} %copy-done.3, f32[32,128,128]{2,1,0:T(8,128)} %data_hbm.1, ...), custom_call_target="tpu_custom_call" | custom-call | flops 6442450944 | bytes 8388608 | tf_op jit(solution)/shard_map/pallas_call | solution.py:189
  26.9 0.0 collective-permute-done.left_hbm
  26.9 0.0 copy-done
  26.9 0.0 copy-done.1
  26.9 0.0 copy-done.2
  26.9 50.3 %shard_map.112 = (f32[2,640,384]{2,1,0:T(8,128)S(1)}, f32[2,512,256]{2,1,0:T(8,128)S(1)}, f32[2,640,384]{2,1,0:T(8,128)S(1)}, f32[256,128]{1,0:T(8,128)S(1)}) custom-call(f32[2,640,384]{2,1,0:T(8,128)S(1)} %copy-done.1, f32[2,640,384]{2,1,0:T(8,128)S(1)} %copy-done.2, f32[2,3,640,128]{3,2,1,0:T(8,128)S(1)} %get-tuple-element.11.grad_hbm, ...), custom_call_target="tpu_custom_call" | custom-call | flops 10000000 | bytes 16777216 | tf_op jit(solution)/shard_map/pallas_call | solution.py:462
  77.3 2.4 %shard_map.113 = (f32[2,640,384]{2,1,0:T(8,128)}, f32[2,512,256]{2,1,0:T(8,128)}, f32[2,640,384]{2,1,0:T(8,128)}, f32[2,128,128]{2,1,0:T(8,128)}) custom-call(f32[2,640,384]{2,1,0:T(8,128)S(1)} %get-tuple-element.14.refs_0_, f32[2,512,256]{2,1,0:T(8,128)S(1)} %get-tuple-element.15.refs_1_, f32[2,640,384]{2,1,0:T(8,128)S(1)} %get-tuple-element.16.refs_2_, ...), custom_call_target="tpu_custom_call" | custom-call | tf_op jit(solution)/shard_map/pallas_call | solution.py:518
Async XLA Ops:
  1.7 25.2 %copy-start = (f32[2,512,256]{2,1,0:T(8,128)S(1)}, f32[2,512,256]{2,1,0:T(8,128)}, u32[]{:S(2)}) copy-start(f32[2,512,256]{2,1,0:T(8,128)} %cons_hbm.1) | copy-start | bytes 3145732
  1.7 25.2 %copy-start.1 = (f32[2,640,384]{2,1,0:T(8,128)S(1)}, f32[2,640,384]{2,1,0:T(8,128)}, u32[]{:S(2)}) copy-start(f32[2,640,384]{2,1,0:T(8,128)} %copy_hbm.3) | copy-start | bytes 5898244
  1.7 25.2 %copy-start.2 = (f32[2,640,384]{2,1,0:T(8,128)S(1)}, f32[2,640,384]{2,1,0:T(8,128)}, u32[]{:S(2)}) copy-start(f32[2,640,384]{2,1,0:T(8,128)} %dual_hbm.1) | copy-start | bytes 5898244
  1.7 25.1 %collective-permute-start = (f32[2,512,128]{2,1,0:T(8,128)S(1)}, f32[2,512,128]{2,1,0:T(8,128)S(1)}, u32[]{:S(2)}, u32[]{:S(2)}) collective-permute-start(f32[2,512,128]{2,1,0:T(8,128)S(1)} %slice.3), channel_id=1, source_target_pairs={{1,0},{2,1},{3,2},{4,3},{5,4},{6,5},{7,6},{8,7},{9,8},{10,9},{11,1... | collective-permute-start | bytes 1572872 | tf_op jit(solution)/shard_map/ppermute | solution.py:530
  8.4 0.9 %copy-start.3 = (f32[2,128,128]{2,1,0:T(8,128)S(1)}, f32[2,128,128]{2,1,0:T(8,128)}, u32[]{:S(2)}) copy-start(f32[2,128,128]{2,1,0:T(8,128)} %probe_hbm.1) | copy-start | bytes 393220
  9.3 0.7 copy-start.4
  10.0 0.7 copy-start.5
  10.6 1.0 %copy-start.6 = (bf16[4,256,256]{2,1,0:T(8,128)(2,1)S(1)}, bf16[4,256,256]{2,1,0:T(8,128)(2,1)}, u32[]{:S(2)}) copy-start(bf16[4,256,256]{2,1,0:T(8,128)(2,1)} %constant.2.clone.tables_hbm) | copy-start | bytes 1572868

commit v3 on v2

v3 whole, which is shorter than its diff:
```python
import functools
import math

import jax
import jax.numpy as jnp
import ml_dtypes
import numpy as np
from jax import lax
from jax.experimental import pallas as pl
from jax.experimental.pallas import tpu as pltpu
from jax.sharding import PartitionSpec as P

MESH = pl.DeviceIdType.MESH
F32 = jnp.float32
BF16 = jnp.bfloat16
SIDE = 128
BATCH = 8

object_step = 0.3
penalty = 1.0
probe_step = 0.5
epsilon = 1e-06


def dft_tables():
    index = np.arange(SIDE)
    angle = 2.0 * np.pi * ((index[:, None] * index[None, :]) % SIDE) / SIDE
    cosine = np.cos(angle) / math.sqrt(SIDE)
    sine = np.sin(angle) / math.sqrt(SIDE)
    forward = np.block([[cosine, -sine], [sine, cosine]])
    backward = np.block([[cosine, sine], [-sine, cosine]])
    parts = []
    for table in (forward, backward):
        high = table.astype(ml_dtypes.bfloat16)
        parts += [high, (table - high.astype(np.float64)).astype(ml_dtypes.bfloat16)]
    return np.stack(parts)


def halves(value):
    high = value.astype(BF16)
    return high, (value - high.astype(F32)).astype(BF16)


def times_right(value, high_table, low_table):
    high, low = halves(value)
    return jnp.dot(
        jnp.concatenate([high, low, high], 1),
        jnp.concatenate([high_table, high_table, low_table], 0),
        preferred_element_type=F32,
    )


def times_left(high_table, low_table, value):
    high, low = halves(value)
    return jnp.dot(
        jnp.concatenate([high_table, low_table, high_table], 1),
        jnp.concatenate([high, high, low], 0),
        preferred_element_type=F32,
    )


def swapped(value):
    s = SIDE
    return jnp.concatenate(
        [
            jnp.concatenate([value[:s, :s], value[s:, :s]], 1),
            jnp.concatenate([value[:s, s:], value[s:, s:]], 1),
        ],
        0,
    )


def step_body(
    n_row, n_col,
    rows_hbm, cols_hbm, copy_hbm, dual_hbm, cons_hbm, probe_hbm, data_hbm, tables_hbm,
    new_copy_ref, new_cons_ref, new_dual_ref, new_probe_ref,
    rows_ref, cols_ref, copy_v, dual_v, cons_v, probe_v, data_v, tables_v,
    terms_v, grad_v, probe_grad_v, w_v,
    from_up, from_down, from_left, from_right,
    col_out, col_in, row_out, row_in, col_all,
    load_sems, halo_send, halo_recv, sum_send, sum_recv,
):
    s = SIDE
    a, b = lax.axis_index("row"), lax.axis_index("col")
    blocks, ext_rows = copy_v.shape[1:3]
    ext_cols = blocks * s
    tile_rows, tile_cols = ext_rows - s, ext_cols - s
    count = data_v.shape[0]
    last = blocks - 1
    lower, upper, middle = pl.ds(tile_rows, s), pl.ds(0, s), pl.ds(s, tile_rows - s)

    pairs = [
        (rows_hbm, rows_ref),
        (cols_hbm, cols_ref),
        (probe_hbm, probe_v),
        (tables_hbm, tables_v),
    ]
    for block in range(blocks):
        pairs.append((copy_hbm.at[:, :, pl.ds(block * s, s)], copy_v.at[:, block]))
    needed = len(pairs)
    for part in range(count // BATCH):
        span = pl.ds(part * BATCH, BATCH)
        pairs.append((data_hbm.at[span], data_v.at[span]))
    early = len(pairs) - count // BATCH + 1
    for block in range(last):
        pairs.append((cons_hbm.at[:, :, pl.ds(block * s, s)], cons_v.at[:, block, pl.ds(0, tile_rows)]))
    pairs.append((dual_hbm, dual_v))
    loads = [
        pltpu.make_async_copy(source, target, load_sems.at[index])
        for index, (source, target) in enumerate(pairs)
    ]
    for load in loads[:early] + loads[-1 - last : -1]:
        load.start()

    def row_peer(index):
        return (index, b)

    def col_peer(index):
        return (a, index)

    barrier = pltpu.get_barrier_semaphore()
    for peer, mine, size in ((row_peer, a, n_row), (col_peer, b, n_col)):

        def greet(hop, carry):
            pl.semaphore_signal(
                barrier, inc=1, device_id=peer(lax.rem(mine + hop, size)), device_id_type=MESH
            )
            return carry

        lax.fori_loop(1, size, greet, 0)

    terms_v[...] = jnp.zeros_like(terms_v)
    grad_v[...] = jnp.zeros_like(grad_v)
    probe_grad_v[...] = jnp.zeros_like(probe_grad_v)

    def remote(source, target, send_sem, recv_sem, device):
        return pltpu.make_async_remote_copy(
            src_ref=source, dst_ref=target, send_sem=send_sem, recv_sem=recv_sem,
            device_id=device, device_id_type=MESH,
        )

    class Spread:
        def __init__(self, phase, peer, mine, size, source_of, slots):
            def move(hop, other):
                return remote(
                    source_of(other), slots.at[mine], sum_send.at[phase, hop], sum_recv.at[phase, hop], peer(other)
                )

            def start(hop, carry):
                move(hop, lax.rem(mine + hop, size)).start()
                return carry

            def arrive(hop, carry):
                other = lax.rem(mine + size - hop, size)
                remote(
                    source_of(other), slots.at[other], sum_send.at[phase, hop], sum_recv.at[phase, hop], peer(other)
                ).wait_recv()
                return carry

            def leave(hop, carry):
                move(hop, lax.rem(mine + hop, size)).wait_send()
                return carry

            lax.fori_loop(1, size, start, 0)
            self.arrived = lambda: lax.fori_loop(1, size, arrive, 0)
            self.left = lambda: lax.fori_loop(1, size, leave, 0)

    class Halo:
        def __init__(self, index, source, target, sends, device, receives):
            move = remote(source, target, halo_send.at[index], halo_recv.at[index], device)
            self.move, self.sends, self.receives = move, sends, receives

        def start(self):
            pl.when(self.sends)(lambda: self.move.start())

        def arrived(self):
            pl.when(self.receives)(lambda: self.move.wait_recv())

        def left(self):
            pl.when(self.sends)(lambda: self.move.wait_send())

    up, down, left, right = (a - 1, b), (a + 1, b), (a, b - 1), (a, b + 1)
    is_up, is_down, is_left, is_right = a > 0, a < n_row - 1, b > 0, b < n_col - 1
    has_up, has_down = is_up.astype(F32), is_down.astype(F32)
    has_left, has_right = is_left.astype(F32), is_right.astype(F32)
    own_rows = pl.ds(0, tile_rows)
    cons_left = Halo(
        0, cons_v.at[:, 0, own_rows], cons_v.at[:, last, own_rows], is_left, left, is_right
    )
    inner = pl.ds(0, last)
    cons_up = Halo(1, cons_v.at[:, inner, upper], cons_v.at[:, inner, lower], is_up, up, is_down)
    cons_corner = Halo(2, cons_v.at[:, last, upper], cons_v.at[:, last, lower], is_up, up, is_down)

    lane = lax.broadcasted_iota(jnp.int32, (s, s), 1)

    def place(member):
        top = rows_ref[member] & (tile_rows - 1)
        left_col = cols_ref[member] & (tile_cols - 1)
        return top, left_col // s, left_col % s

    def collect(batch):
        spots = [place(batch * BATCH + member) for member in range(BATCH)]
        for first in range(0, ext_rows, s):
            span = pl.ds(first, s)
            rows = [jnp.clip(first - top, -s, s) + s for top, _, _ in spots]
            for part in range(2):
                for block in range(blocks):
                    total = grad_v[part, block, span, :]
                    for member in range(BATCH):
                        _, home, _ = spots[member]
                        kind = jnp.clip(block - home, 0, 1)
                        row = jnp.where(kind == block - home, rows[member], 0)
                        total = total + terms_v[kind, member, part, pl.ds(row, s), :]
                    grad_v[part, block, span, :] = total

    for load in loads[:needed]:
        load.wait()
    for load in loads[early : early + count // BATCH - 1] + loads[-1:]:
        load.start()

    def work(index, carry):
        loads_data(index).wait()

        collect(jnp.maximum(index - 1, 0))

        @pl.when(index == 1)
        def _():
            pl.semaphore_wait(barrier, n_row + n_col - 2)
            for load in loads[-1 - last : -1]:
                load.wait()
            cons_up.start()
            cons_left.start()

        forward = (tables_v[0], tables_v[1])
        backward = (tables_v[2], tables_v[3])
        probe_re, probe_im = probe_v[0], probe_v[1]
        spots, fields = [], []
        for member in range(BATCH):
            top, block, shift = place(index * BATCH + member)
            spots.append(shift)
            field = []
            for part in range(2):
                near = copy_v[part, block, pl.ds(top, s), :]
                far = copy_v[part, block + 1, pl.ds(top, s), :]
                field.append(pltpu.roll(jnp.where(lane >= shift, near, far), (s - shift) % s, 1))
            fields.append(field)
        sum_re = jnp.zeros((s, s), F32)
        sum_im = jnp.zeros((s, s), F32)
        waves = []
        for re, im in fields:
            waves.append(
                jnp.concatenate([probe_re * re - probe_im * im, probe_re * im + probe_im * re], 1)
            )
        rows_done = times_right(jnp.concatenate(waves, 0), *forward)
        misfits = []
        for first in range(0, BATCH, 2):
            spectrum = times_left(*backward, swapped(rows_done[first * s : (first + 2) * s]))
            spec_re, spec_im = spectrum[:s], spectrum[s:]
            data = jnp.concatenate(
                [data_v[index * BATCH + first], data_v[index * BATCH + first + 1]], 1
            )
            residue = spec_re * spec_re + spec_im * spec_im - data
            weighted = jnp.concatenate([residue * spec_re, residue * spec_im], 0)
            misfits.append(swapped(times_left(*forward, weighted)))
        misfit = times_right(jnp.concatenate(misfits, 0), *backward)
        for member in range(BATCH):
            mis_re = misfit[member * s : (member + 1) * s, :s]
            mis_im = misfit[member * s : (member + 1) * s, s:]
            re, im = fields[member]
            sum_re += re * mis_re + im * mis_im
            sum_im += re * mis_im - im * mis_re
            shift = spots[member]
            terms = (probe_re * mis_re + probe_im * mis_im, probe_re * mis_im - probe_im * mis_re)
            for part in range(2):
                term = pltpu.roll(terms[part], shift, 1)
                terms_v[0, member, part, pl.ds(s, s), :] = jnp.where(lane >= shift, term, 0.0)
                terms_v[1, member, part, pl.ds(s, s), :] = jnp.where(lane >= shift, 0.0, term)
        probe_grad_v[0] += sum_re
        probe_grad_v[1] += sum_im
        return carry

    def loads_data(index):
        span = pl.ds(index * BATCH, BATCH)
        return pltpu.make_async_copy(data_hbm.at[span], data_v.at[span], load_sems.at[needed + index])

    lax.fori_loop(0, count // BATCH, work, 0)
    collect(count // BATCH - 1)

    def squares(index, total):
        for part in range(2):
            for block in range(blocks):
                value = grad_v[part, block, pl.ds(pl.multiple_of(index * 8, 8), 8), :]
                total = total + value * value
        return total

    norm = lax.fori_loop(0, ext_rows // 8, squares, jnp.zeros((8, s), F32))

    piece = col_out.shape[1] - 8
    for index in range(n_col):
        first = index * piece
        col_out[index, :piece] = probe_grad_v[first // s, pl.ds(first % s, piece), :]
        col_out[index, piece:] = norm
    first_sum = Spread(0, col_peer, b, n_col, lambda other: col_out.at[other], col_in)
    col_in[b] = col_out[b]

    loads[-1].wait()

    first_sum.arrived()

    def total_of(slots, size):
        total = slots[0]
        for index in range(1, size):
            total = total + slots[index]
        return total

    row_out[...] = total_of(col_in, n_col)
    second_sum = Spread(1, row_peer, a, n_row, lambda other: row_out, row_in)
    row_in[a] = row_out[...]
    second_sum.arrived()
    whole = total_of(row_in, n_row)
    total_squares = jnp.sum(whole[piece:], keepdims=True)
    scale = object_step / jnp.sqrt(total_squares / (n_row * n_col * ext_rows * ext_cols) + epsilon)
    keep = 1.0 - object_step * penalty
    pull = object_step * penalty

    def fill(first, size, block):
        columns = pl.ds(block * s, s)
        span = pl.ds(first, size)
        for part in range(2):
            old, dual = copy_v[part, block, span], dual_v[part, span, columns]
            w_v[part, block, span, :] = keep * (old + dual) - scale * grad_v[part, block, span, :]

    order = [(part, block) for block in [0, last] + list(range(1, last)) for part in range(2)]
    rows_up, rows_down = {}, {}
    for index, (part, block) in enumerate(order):
        rows_up[part, block] = Halo(
            3 + index, w_v.at[part, block, upper], from_down.at[part, block], is_up, up, is_down
        )
        rows_down[part, block] = Halo(
            3 + len(order) + index, w_v.at[part, block, lower], from_up.at[part, block], is_down, down, is_up
        )
    used = 3 + 2 * len(order)
    half, edge = n_col // 2, n_col - 1
    via_last, via_first = (b == half) & (n_col > 2), (b == half - 1) & (n_col > 2)
    mids = [
        Halo(used, w_v.at[0, 0, middle], from_right.at[0, middle], is_left, left, is_right),
        Halo(used + 1, w_v.at[0, last, middle], from_left.at[0, middle], is_right, right, is_left),
        Halo(
            used + 2, w_v.at[1, 0, middle], from_right.at[1, middle],
            is_left, (a, jnp.where(via_last, edge, b - 1)), is_right,
        ),
        Halo(
            used + 3, w_v.at[1, last, middle], from_left.at[1, middle],
            is_right, (a, jnp.where(via_first, 0, b + 1)), is_left,
        ),
    ]
    passed = [
        Halo(used + 2, from_right.at[1, middle], from_right.at[1, middle], b == edge, (a, half - 1), False),
        Halo(used + 3, from_left.at[1, middle], from_left.at[1, middle], b == 0, (a, half), False),
    ]
    used += 4
    corners = {}
    for part in range(2):
        for block, target, sends, device, receives in (
            (0, from_right, is_left, left, is_right),
            (last, from_left, is_right, right, is_left),
        ):
            for source, span in ((from_up, upper), (from_down, lower)):
                corners[part, block, span is upper] = Halo(
                    used, source.at[part, block], target.at[part, span], sends, device, receives
                )
                used += 1
    col_all[b] = whole[:piece]
    third_sum = Spread(2, col_peer, b, n_col, lambda other: col_all.at[b], col_all)
    for block in (0, last):
        fill(0, s, block)
        fill(tile_rows, s, block)
        for part in range(2):
            rows_up[part, block].start()
            rows_down[part, block].start()
    fill(s, tile_rows - s, 0)
    mids[2].start()
    mids[0].start()
    fill(s, tile_rows - s, last)
    mids[3].start()
    mids[1].start()
    for block in range(1, last):
        fill(0, s, block)
        fill(tile_rows, s, block)
        for part in range(2):
            rows_up[part, block].start()
            rows_down[part, block].start()
    for block in range(1, last):
        fill(s, tile_rows - s, block)

    def neighbour(present, value):
        return jnp.where(present, value, 0.0)

    def join(part, block):
        rows_up[part, block].arrived()
        rows_down[part, block].arrived()
        from_up[part, block] = w_v[part, block, upper] + neighbour(is_up, from_up[part, block])
        from_down[part, block] = w_v[part, block, lower] + neighbour(is_down, from_down[part, block])

    for block in (0, last):
        for part in range(2):
            join(part, block)
            corners[part, block, True].start()
            corners[part, block, False].start()

    if n_col > 2:
        for flag, move, onward in ((b == edge, mids[2], passed[0]), (b == 0, mids[3], passed[1])):

            @pl.when(flag)
            def _():
                move.move.wait_recv()
                onward.move.start()

    cons_left.arrived()
    pl.when(jnp.logical_not(is_right))(
        lambda: cons_v.__setitem__((slice(None), last, own_rows), jnp.zeros((2, tile_rows, s), F32))
    )
    cons_corner.start()
    pl.when(jnp.logical_not(is_down))(
        lambda: cons_v.__setitem__((slice(None), slice(None), lower), jnp.zeros((2, blocks, s, s), F32))
    )
    cons_up.arrived()

    def renew(span, block):
        columns = pl.ds(block * s, s)
        for part in range(2):
            new_copy_ref[part, span, columns] = (
                w_v[part, block, span] - dual_v[part, span, columns] + pull * cons_v[part, block, span]
            )

    for block in range(blocks):
        renew(own_rows, block)
        if block < last:
            renew(lower, block)
    for part in range(2):
        for block in range(1, last):
            columns = pl.ds(block * s, s)
            new_cons_ref[part, middle, columns] = w_v[part, block, middle] + pull * cons_v[part, block, middle]
            new_dual_ref[part, middle, columns] = jnp.zeros((tile_rows - s, s), F32)

    def finish(span, block, total, cover_rows, inside_rows):
        columns = pl.ds(block * s, s)
        for part in range(2):
            summed = total(part)
            cover = cover_rows
            inside = inside_rows
            if block == 0:
                summed = summed + neighbour(is_left, from_left[part, span])
                cover = cover * (1.0 + has_left)
            if block == last:
                summed = summed + neighbour(is_right, from_right[part, span])
                cover = cover * (1.0 + has_right)
                inside = inside * has_right
            mean = summed * (1.0 / cover)
            new_dual_ref[part, span, columns] = w_v[part, block, span] - inside * mean
            if block < last and span is not lower:
                new_cons_ref[part, span, columns] = mean + pull * cons_v[part, block, span]

    one = jnp.float32(1.0)

    def top_and_bottom(block):
        finish(upper, block, lambda part: from_up[part, block], 1.0 + has_up, one)
        finish(lower, block, lambda part: from_down[part, block], 1.0 + has_down, has_down)

    for block in range(1, last):
        for part in range(2):
            join(part, block)
        top_and_bottom(block)
    mids[0].arrived()
    mids[1].arrived()
    mids[2].arrived()
    mids[3].arrived()
    for block in (0, last):
        finish(middle, block, lambda part: w_v[part, block, middle], one, one)

    third_sum.arrived()
    power = jnp.zeros((piece, s), F32)
    for index in range(n_col):
        power = power + col_all[index] * col_all[index]
    rate = probe_step / jnp.sqrt(jnp.sum(power, keepdims=True) / (s * s) + epsilon)
    for index in range(n_col):
        first = index * piece
        half, span = first // s, pl.ds(first % s, piece)
        new_probe_ref[half, span, :] = probe_v[half, span, :] - rate * col_all[index]

    cons_corner.arrived()
    renew(lower, last)
    for corner in corners.values():
        corner.arrived()
    for block in (0, last):
        top_and_bottom(block)

    halos = [cons_left, cons_up, cons_corner] + mids + (passed if n_col > 2 else [])
    for group in (rows_up, rows_down, corners):
        halos += list(group.values())
    for move in halos + [first_sum, second_sum, third_sum]:
        move.left()


def step(n_row, n_col, pos_rows, pos_cols, local_copy, dual, consensus, probe, intensity):
    s = SIDE
    count = intensity.shape[0]
    ext_rows, ext_cols = local_copy.shape[1:]
    blocks = ext_cols // s
    piece = 2 * s // n_col
    vmem, hbm = pl.BlockSpec(memory_space=pltpu.VMEM), pl.BlockSpec(memory_space=pltpu.HBM)
    halos = 3 + 4 * blocks + 4 + 8
    return pl.pallas_call(
        functools.partial(step_body, n_row, n_col),
        in_specs=[hbm] * 8,
        out_specs=[vmem] * 4,
        out_shape=[
            jax.ShapeDtypeStruct(local_copy.shape, F32),
            jax.ShapeDtypeStruct(consensus.shape, F32),
            jax.ShapeDtypeStruct(local_copy.shape, F32),
            jax.ShapeDtypeStruct(probe.shape, F32),
        ],
        scratch_shapes=[
            pltpu.SMEM(pos_rows.shape, jnp.int32),
            pltpu.SMEM(pos_cols.shape, jnp.int32),
            pltpu.VMEM((2, blocks, ext_rows, s), F32),
            pltpu.VMEM(dual.shape, F32),
            pltpu.VMEM((2, blocks, ext_rows, s), F32),
            pltpu.VMEM(probe.shape, F32),
            pltpu.VMEM(intensity.shape, F32),
            pltpu.VMEM((4, 2 * s, 2 * s), BF16),
            pltpu.VMEM((2, BATCH, 2, 3 * s, s), F32),
            pltpu.VMEM((2, blocks, ext_rows, s), F32),
            pltpu.VMEM((2, s, s), F32),
            pltpu.VMEM((2, blocks, ext_rows, s), F32),
            pltpu.VMEM((2, blocks, s, s), F32),
            pltpu.VMEM((2, blocks, s, s), F32),
            pltpu.VMEM((2, ext_rows, s), F32),
            pltpu.VMEM((2, ext_rows, s), F32),
            pltpu.VMEM((n_col, piece + 8, s), F32),
            pltpu.VMEM((n_col, piece + 8, s), F32),
            pltpu.VMEM((piece + 8, s), F32),
            pltpu.VMEM((n_row, piece + 8, s), F32),
            pltpu.VMEM((n_col, piece, s), F32),
            pltpu.SemaphoreType.DMA((4 + blocks + count // BATCH + blocks,)),
            pltpu.SemaphoreType.DMA((halos,)),
            pltpu.SemaphoreType.DMA((halos,)),
            pltpu.SemaphoreType.DMA((3, max(n_row, n_col))),
            pltpu.SemaphoreType.DMA((3, max(n_row, n_col))),
        ],
        compiler_params=pltpu.CompilerParams(
            collective_id=0, has_side_effects=True, vmem_limit_bytes=46 * 2**20
        ),
        cost_estimate=pl.CostEstimate(
            flops=count * 4 * 3 * 2 * s * 256 * 256, bytes_accessed=16 * 2**20, transcendentals=0
        ),
    )(pos_rows, pos_cols, local_copy, dual, consensus, probe, intensity, jnp.asarray(dft_tables()))


def store_body(*refs):
    count = len(refs) // 2
    sources, targets, sems = refs[:count], refs[count : 2 * count], refs[2 * count]
    moves = [
        pltpu.make_async_copy(source.at[part], target.at[part], sems.at[index, part])
        for index, (source, target) in enumerate(zip(sources, targets))
        for part in range(2)
    ]
    for move in moves:
        move.start()
    for move in moves:
        move.wait()


def store(*arrays):
    return pl.pallas_call(
        store_body,
        in_specs=[pl.BlockSpec(memory_space=pltpu.VMEM)] * len(arrays),
        out_specs=[pl.BlockSpec(memory_space=pl.ANY)] * len(arrays),
        out_shape=[jax.ShapeDtypeStruct(array.shape, F32) for array in arrays],
        scratch_shapes=[pltpu.SemaphoreType.DMA((len(arrays), 2))],
        compiler_params=pltpu.CompilerParams(vmem_limit_bytes=16 * 2**20),
    )(*arrays)


def per_device(n_row, n_col, local_copy, dual, consensus, probe, intensity, pos_rows, pos_cols):
    new_copy, new_consensus, new_dual, new_probe = step(
        n_row, n_col, pos_rows, pos_cols, local_copy, dual, consensus, probe, intensity
    )
    return tuple(store(new_copy, new_consensus, new_dual, new_probe))


def solution(mesh):
    field = P(None, "row", "col")
    both = ("row", "col")
    return jax.shard_map(
        functools.partial(per_device, mesh.shape["row"], mesh.shape["col"]),
        mesh=mesh,
        in_specs=(field, field, field, P(), P(both, None, None), P(both), P(both)),
        out_specs=(field, field, field, P()),
        check_vma=False,
    )
```

time: 79.9 us -> 73.2 us (0.916)
  starting transfers between devices: 6.65 us -> 0 us
    ppermute x1 -> x0, starting transfers between devices: 6.65 us -> none  [per_device(): lax.ppermute(consensus[:, :, :s], 'col', [(j, j - 1) for j in range(1, n_...]
    unnamed x14 -> x10, local copies, waits for them, and re-layouts: 3.27 us -> 4.47 us
    slice x1 -> x0, local copies, waits for them, and re-layouts: 1.08 us -> none  [per_device(): consensus[:, :, :s]]
    pallas_call x2 -> x1, Pallas kernels: 65.6 us -> 65.5 us  [step(): pl.pallas_call(functools.partial(step_body, n_row, n_col), in_specs=[hbm]...]
  transfers between devices with their start and end apart: 1 -> 0, of which waited for: 0 -> 0; matrix products, arithmetic and copies ran while one was open for 0% -> 0% of each run, Pallas kernels for 19% -> 0%
where the time goes in v3:
time: 73.2 us; the launch traced here: 73 us
  Pallas kernels  67.9 us (93%)
  local copies, waits for them, and re-layouts  4.47 us (6%)
    pallas_call x1, Pallas kernels, step(): pl.pallas_call(functools.partial(step_body, n_row, n_col), in_specs=[hbm]...  65.5 us
    unnamed x10, local copies, waits for them, and re-layouts  4.47 us
    pallas_call x1, Pallas kernels, store(): pl.pallas_call(store_body, in_specs=[pl.BlockSpec(memory_space=pltpu.VMEM...  2.36 us

profile of v3, /device:TPU:33, one launch (start us, length us, event | category | flops | bytes accessed | tf_op | source)
XLA Modules:
  0.0 73.0 jit_solution(15113891902727892460)
XLA Ops:
  0.6 0.0 copy-start
  0.6 1.2 %copy-done = f32[2,512,256]{2,1,0:T(8,128)S(1)} copy-done((f32[2,512,256]{2,1,0:T(8,128)S(1)}, f32[2,512,256]{2,1,0:T(8,128)}, u32[]{:S(2)}) %copy-start) | copy-done | bytes 1048600
  1.9 0.0 copy-start.1
  1.9 0.9 %copy-done.1 = f32[2,128,128]{2,1,0:T(8,128)S(1)} copy-done((f32[2,128,128]{2,1,0:T(8,128)S(1)}, f32[2,128,128]{2,1,0:T(8,128)}, u32[]{:S(2)}) %copy-start.1) | copy-done | bytes 131096
  2.8 0.0 copy-start.2
  2.8 0.7 copy-done.2
  3.4 0.0 copy-start.3
  3.4 0.7 copy-done.3
  4.1 0.0 copy-start.4
  4.1 1.0 %copy-done.4 = bf16[4,256,256]{2,1,0:T(8,128)(2,1)S(1)} copy-done((bf16[4,256,256]{2,1,0:T(8,128)(2,1)S(1)}, bf16[4,256,256]{2,1,0:T(8,128)(2,1)}, u32[]{:S(2)}) %copy-start.4) | copy-done | bytes 524312
  5.1 65.5 %shard_map.111 = (f32[2,640,384]{2,1,0:T(8,128)S(1)}, f32[2,512,256]{2,1,0:T(8,128)S(1)}, f32[2,640,384]{2,1,0:T(8,128)S(1)}, f32[2,128,128]{2,1,0:T(8,128)S(1)}) custom-call(s32[32]{0:T(128)S(1)} %copy-done.2, s32[32]{0:T(128)S(1)} %copy-done.3, f32[2,640,384]{2,1,0:T(8,128)} %copy_hbm.1, f32[2,640,384]{2,1,0:T(8,128)} %dual_hbm.1, ...), custom_call_target="tpu_custom_call" | custom-call | flops 6442450944 | bytes 16777216 | tf_op jit(solution)/shard_map/pallas_call | solution.py:513
  70.6 2.4 %shard_map.112 = (f32[2,640,384]{2,1,0:T(8,128)}, f32[2,512,256]{2,1,0:T(8,128)}, f32[2,640,384]{2,1,0:T(8,128)}, f32[2,128,128]{2,1,0:T(8,128)}) custom-call(f32[2,640,384]{2,1,0:T(8,128)S(1)} %get-tuple-element.8.refs_0_, f32[2,512,256]{2,1,0:T(8,128)S(1)} %get-tuple-element.9.refs_1_, f32[2,640,384]{2,1,0:T(8,128)S(1)} %get-tuple-element.10.refs_2_, ...), custom_call_target="tpu_custom_call" | custom-call | tf_op jit(solution)/shard_map/pallas_call | solution.py:575
Async XLA Ops:
  0.6 1.2 %copy-start = (f32[2,512,256]{2,1,0:T(8,128)S(1)}, f32[2,512,256]{2,1,0:T(8,128)}, u32[]{:S(2)}) copy-start(f32[2,512,256]{2,1,0:T(8,128)} %cons_hbm.1) | copy-start | bytes 3145732
  1.9 0.9 %copy-start.1 = (f32[2,128,128]{2,1,0:T(8,128)S(1)}, f32[2,128,128]{2,1,0:T(8,128)}, u32[]{:S(2)}) copy-start(f32[2,128,128]{2,1,0:T(8,128)} %probe_hbm.1) | copy-start | bytes 393220
  2.8 0.7 copy-start.2
  3.4 0.7 copy-start.3
  4.1 1.0 %copy-start.4 = (bf16[4,256,256]{2,1,0:T(8,128)(2,1)S(1)}, bf16[4,256,256]{2,1,0:T(8,128)(2,1)}, u32[]{:S(2)}) copy-start(bf16[4,256,256]{2,1,0:T(8,128)(2,1)} %constant.2.clone.tables_hbm) | copy-start | bytes 1572868

commit v4 on v3

--- a/solution.py
+++ b/solution.py
@@ -3,8 +3,6 @@
 
 import jax
 import jax.numpy as jnp
-import ml_dtypes
-import numpy as np
 from jax import lax
 from jax.experimental import pallas as pl
 from jax.experimental.pallas import tpu as pltpu
@@ -22,18 +20,25 @@
 epsilon = 1e-06
 
 
-def dft_tables():
-    index = np.arange(SIDE)
-    angle = 2.0 * np.pi * ((index[:, None] * index[None, :]) % SIDE) / SIDE
-    cosine = np.cos(angle) / math.sqrt(SIDE)
-    sine = np.sin(angle) / math.sqrt(SIDE)
-    forward = np.block([[cosine, -sine], [sine, cosine]])
-    backward = np.block([[cosine, sine], [-sine, cosine]])
-    parts = []
-    for table in (forward, backward):
-        high = table.astype(ml_dtypes.bfloat16)
-        parts += [high, (table - high.astype(np.float64)).astype(ml_dtypes.bfloat16)]
-    return np.stack(parts)
+def fill_tables(tables_ref):
+    row = lax.broadcasted_iota(jnp.int32, (SIDE, SIDE), 0)
+    column = lax.broadcasted_iota(jnp.int32, (SIDE, SIDE), 1)
+    turn = ((row * column + SIDE // 2) & (SIDE - 1)) - SIDE // 2
+    angle = turn.astype(F32) * (math.pi / SIDE)
+    square = angle * angle
+    half_sine, half_cosine = jnp.zeros_like(angle), jnp.zeros_like(angle)
+    for order in range(8, -1, -1):
+        half_sine = half_sine * square + (-1.0) ** order / math.factorial(2 * order + 1)
+        half_cosine = half_cosine * square + (-1.0) ** order / math.factorial(2 * order)
+    half_sine = half_sine * angle
+    norm = 1.0 / math.sqrt(SIDE)
+    cosine = norm - (2.0 * norm) * half_sine * half_sine
+    sine = (2.0 * norm) * half_sine * half_cosine
+    for index, signed in enumerate((sine, -sine)):
+        table = jnp.concatenate([jnp.concatenate([cosine, -signed], 1), jnp.concatenate([signed, cosine], 1)], 0)
+        high, low = halves(table)
+        tables_ref[2 * index] = high
+        tables_ref[2 * index + 1] = low
 
 
 def halves(value):
@@ -72,7 +77,7 @@
 
 def step_body(
     n_row, n_col,
-    rows_hbm, cols_hbm, copy_hbm, dual_hbm, cons_hbm, probe_hbm, data_hbm, tables_hbm,
+    rows_hbm, cols_hbm, copy_hbm, dual_hbm, cons_hbm, probe_hbm, data_hbm,
     new_copy_ref, new_cons_ref, new_dual_ref, new_probe_ref,
     rows_ref, cols_ref, copy_v, dual_v, cons_v, probe_v, data_v, tables_v,
     terms_v, grad_v, probe_grad_v, w_v,
@@ -93,7 +98,6 @@
         (rows_hbm, rows_ref),
         (cols_hbm, cols_ref),
         (probe_hbm, probe_v),
-        (tables_hbm, tables_v),
     ]
     for block in range(blocks):
         pairs.append((copy_hbm.at[:, :, pl.ds(block * s, s)], copy_v.at[:, block]))
@@ -129,6 +133,7 @@
 
         lax.fori_loop(1, size, greet, 0)
 
+    fill_tables(tables_v)
     terms_v[...] = jnp.zeros_like(terms_v)
     grad_v[...] = jnp.zeros_like(grad_v)
     probe_grad_v[...] = jnp.zeros_like(probe_grad_v)
@@ -221,7 +226,7 @@
     def work(index, carry):
         loads_data(index).wait()
 
-        collect(jnp.maximum(index - 1, 0))
+        pl.when(index > 0)(lambda: collect(index - 1))
 
         @pl.when(index == 1)
         def _():
@@ -341,24 +346,46 @@
         )
     used = 3 + 2 * len(order)
     half, edge = n_col // 2, n_col - 1
-    via_last, via_first = (b == half) & (n_col > 2), (b == half - 1) & (n_col > 2)
-    mids = [
-        Halo(used, w_v.at[0, 0, middle], from_right.at[0, middle], is_left, left, is_right),
-        Halo(used + 1, w_v.at[0, last, middle], from_left.at[0, middle], is_right, right, is_left),
-        Halo(
-            used + 2, w_v.at[1, 0, middle], from_right.at[1, middle],
-            is_left, (a, jnp.where(via_last, edge, b - 1)), is_right,
-        ),
-        Halo(
-            used + 3, w_v.at[1, last, middle], from_left.at[1, middle],
-            is_right, (a, jnp.where(via_first, 0, b + 1)), is_left,
-        ),
+    relays = n_col > 2
+    via_last, via_first = (b == half) & relays, (b == half - 1) & relays
+    size = tile_rows - s
+    pieces = [
+        (1, pl.ds(s, size), True),
+        (0, pl.ds(s, size // 2), True),
+        (0, pl.ds(s + size // 2, size // 2), False),
     ]
-    passed = [
-        Halo(used + 2, from_right.at[1, middle], from_right.at[1, middle], b == edge, (a, half - 1), False),
-        Halo(used + 3, from_left.at[1, middle], from_left.at[1, middle], b == 0, (a, half), False),
-    ]
-    used += 4
+    to_left, to_right, onward_left, onward_right = [], [], [], []
+    for part, span, relayed in pieces:
+        target_left, target_right = b - 1, b + 1
+        if relayed:
+            target_left = jnp.where(via_last, edge, b - 1)
+            target_right = jnp.where(via_first, 0, b + 1)
+            onward_left.append(
+                Halo(used, from_right.at[part, span], from_right.at[part, span], b == edge, (a, half - 1), False)
+            )
+            onward_right.append(
+                Halo(used + 1, from_left.at[part, span], from_left.at[part, span], b == 0, (a, half), False)
+            )
+        to_left.append(
+            Halo(used, w_v.at[part, 0, span], from_right.at[part, span], is_left, (a, target_left), is_right)
+        )
+        to_right.append(
+            Halo(used + 1, w_v.at[part, last, span], from_left.at[part, span], is_right, (a, target_right), is_left)
+        )
+        used += 2
+
+    def relay(index):
+        if relays:
+            for flag, move, onward in (
+                (b == edge, to_left[index], onward_left[index]),
+                (b == 0, to_right[index], onward_right[index]),
+            ):
+
+                @pl.when(flag)
+                def _():
+                    move.move.wait_recv()
+                    onward.move.start()
+
     corners = {}
     for part in range(2):
         for block, target, sends, device, receives in (
@@ -379,11 +406,11 @@
             rows_up[part, block].start()
             rows_down[part, block].start()
     fill(s, tile_rows - s, 0)
-    mids[2].start()
-    mids[0].start()
+    for move in to_left:
+        move.start()
     fill(s, tile_rows - s, last)
-    mids[3].start()
-    mids[1].start()
+    for move in to_right:
+        move.start()
     for block in range(1, last):
         fill(0, s, block)
         fill(tile_rows, s, block)
@@ -402,19 +429,14 @@
         from_up[part, block] = w_v[part, block, upper] + neighbour(is_up, from_up[part, block])
         from_down[part, block] = w_v[part, block, lower] + neighbour(is_down, from_down[part, block])
 
+    relay(0)
     for block in (0, last):
         for part in range(2):
             join(part, block)
             corners[part, block, True].start()
             corners[part, block, False].start()
 
-    if n_col > 2:
-        for flag, move, onward in ((b == edge, mids[2], passed[0]), (b == 0, mids[3], passed[1])):
-
-            @pl.when(flag)
-            def _():
-                move.move.wait_recv()
-                onward.move.start()
+    relay(1)
 
     cons_left.arrived()
     pl.when(jnp.logical_not(is_right))(
@@ -471,10 +493,8 @@
         for part in range(2):
             join(part, block)
         top_and_bottom(block)
-    mids[0].arrived()
-    mids[1].arrived()
-    mids[2].arrived()
-    mids[3].arrived()
+    for move in to_left + to_right:
+        move.arrived()
     for block in (0, last):
         finish(middle, block, lambda part: w_v[part, block, middle], one, one)
 
@@ -495,7 +515,7 @@
     for block in (0, last):
         top_and_bottom(block)
 
-    halos = [cons_left, cons_up, cons_corner] + mids + (passed if n_col > 2 else [])
+    halos = [cons_left, cons_up, cons_corner] + to_left + to_right + (onward_left + onward_right if relays else [])
     for group in (rows_up, rows_down, corners):
         halos += list(group.values())
     for move in halos + [first_sum, second_sum, third_sum]:
@@ -509,10 +529,10 @@
     blocks = ext_cols // s
     piece = 2 * s // n_col
     vmem, hbm = pl.BlockSpec(memory_space=pltpu.VMEM), pl.BlockSpec(memory_space=pltpu.HBM)
-    halos = 3 + 4 * blocks + 4 + 8
+    halos = 3 + 4 * blocks + 6 + 8
     return pl.pallas_call(
         functools.partial(step_body, n_row, n_col),
-        in_specs=[hbm] * 8,
+        in_specs=[hbm] * 7,
         out_specs=[vmem] * 4,
         out_shape=[
             jax.ShapeDtypeStruct(local_copy.shape, F32),
@@ -542,7 +562,7 @@
             pltpu.VMEM((piece + 8, s), F32),
             pltpu.VMEM((n_row, piece + 8, s), F32),
             pltpu.VMEM((n_col, piece, s), F32),
-            pltpu.SemaphoreType.DMA((4 + blocks + count // BATCH + blocks,)),
+            pltpu.SemaphoreType.DMA((3 + blocks + count // BATCH + blocks,)),
             pltpu.SemaphoreType.DMA((halos,)),
             pltpu.SemaphoreType.DMA((halos,)),
             pltpu.SemaphoreType.DMA((3, max(n_row, n_col))),
@@ -554,7 +574,7 @@
         cost_estimate=pl.CostEstimate(
             flops=count * 4 * 3 * 2 * s * 256 * 256, bytes_accessed=16 * 2**20, transcendentals=0
         ),
-    )(pos_rows, pos_cols, local_copy, dual, consensus, probe, intensity, jnp.asarray(dft_tables()))
+    )(pos_rows, pos_cols, local_copy, dual, consensus, probe, intensity)
 
 
 def store_body(*refs):

time: 73.2 us -> 70.2 us (0.959)
  Pallas kernels: 67.9 us -> 64.4 us
    pallas_call x1, Pallas kernels: 65.5 us -> 62 us  [step(): pl.pallas_call(functools.partial(step_body, n_row, n_col), in_specs=[hbm]...]
where the time goes in v4:
time: 70.2 us; the launch traced here: 70 us
  Pallas kernels  64.4 us (92%)
  local copies, waits for them, and re-layouts  4.98 us (7%)
    pallas_call x1, Pallas kernels, step(): pl.pallas_call(functools.partial(step_body, n_row, n_col), in_specs=[hbm]...  62 us
    unnamed x10, local copies, waits for them, and re-layouts  4.98 us
    pallas_call x1, Pallas kernels, store(): pl.pallas_call(store_body, in_specs=[pl.BlockSpec(memory_space=pltpu.VMEM...  2.36 us

profile of v4, /device:TPU:33, one launch (start us, length us, event | category | flops | bytes accessed | tf_op | source)
XLA Modules:
  0.0 70.0 jit_solution(14603111738942997221)
XLA Ops:
  0.6 0.0 copy-start
  0.6 1.5 %copy-done = f32[2,640,384]{2,1,0:T(8,128)S(1)} copy-done((f32[2,640,384]{2,1,0:T(8,128)S(1)}, f32[2,640,384]{2,1,0:T(8,128)}, u32[]{:S(2)}) %copy-start) | copy-done | bytes 1966104
  2.2 0.0 copy-start.1
  2.2 1.2 %copy-done.1 = f32[2,512,256]{2,1,0:T(8,128)S(1)} copy-done((f32[2,512,256]{2,1,0:T(8,128)S(1)}, f32[2,512,256]{2,1,0:T(8,128)}, u32[]{:S(2)}) %copy-start.1) | copy-done | bytes 1048600
  3.4 0.0 copy-start.2
  3.4 0.9 %copy-done.2 = f32[2,128,128]{2,1,0:T(8,128)S(1)} copy-done((f32[2,128,128]{2,1,0:T(8,128)S(1)}, f32[2,128,128]{2,1,0:T(8,128)}, u32[]{:S(2)}) %copy-start.2) | copy-done | bytes 131096
  4.3 0.0 copy-start.3
  4.3 0.7 copy-done.3
  5.0 0.0 copy-start.4
  5.0 0.7 copy-done.4
  5.6 62.0 %shard_map.102 = (f32[2,640,384]{2,1,0:T(8,128)S(1)}, f32[2,512,256]{2,1,0:T(8,128)S(1)}, f32[2,640,384]{2,1,0:T(8,128)S(1)}, f32[2,128,128]{2,1,0:T(8,128)S(1)}) custom-call(s32[32]{0:T(128)S(1)} %copy-done.3, s32[32]{0:T(128)S(1)} %copy-done.4, f32[2,640,384]{2,1,0:T(8,128)S(1)} %copy-done, f32[2,640,384]{2,1,0:T(8,128)} %dual_hbm.1, ...), custom_call_target="tpu_custom_call" | custom-call | flops 6442450944 | bytes 16777216 | tf_op jit(solution)/shard_map/pallas_call | solution.py:533
  67.6 2.4 %shard_map.103 = (f32[2,640,384]{2,1,0:T(8,128)}, f32[2,512,256]{2,1,0:T(8,128)}, f32[2,640,384]{2,1,0:T(8,128)}, f32[2,128,128]{2,1,0:T(8,128)}) custom-call(f32[2,640,384]{2,1,0:T(8,128)S(1)} %get-tuple-element.8.refs_0_, f32[2,512,256]{2,1,0:T(8,128)S(1)} %get-tuple-element.9.refs_1_, f32[2,640,384]{2,1,0:T(8,128)S(1)} %get-tuple-element.10.refs_2_, ...), custom_call_target="tpu_custom_call" | custom-call | tf_op jit(solution)/shard_map/pallas_call | solution.py:595
Async XLA Ops:
  0.6 1.5 %copy-start = (f32[2,640,384]{2,1,0:T(8,128)S(1)}, f32[2,640,384]{2,1,0:T(8,128)}, u32[]{:S(2)}) copy-start(f32[2,640,384]{2,1,0:T(8,128)} %copy_hbm.1) | copy-start | bytes 5898244
  2.2 1.2 %copy-start.1 = (f32[2,512,256]{2,1,0:T(8,128)S(1)}, f32[2,512,256]{2,1,0:T(8,128)}, u32[]{:S(2)}) copy-start(f32[2,512,256]{2,1,0:T(8,128)} %cons_hbm.1) | copy-start | bytes 3145732
  3.4 0.9 %copy-start.2 = (f32[2,128,128]{2,1,0:T(8,128)S(1)}, f32[2,128,128]{2,1,0:T(8,128)}, u32[]{:S(2)}) copy-start(f32[2,128,128]{2,1,0:T(8,128)} %probe_hbm.1) | copy-start | bytes 393220
  4.3 0.7 copy-start.3
  5.0 0.7 copy-start.4
